TPU v7x, 128 devices: a whole 4x4x4 slice. The times are simulated.
128 devices in a mesh: fsdp: 32 (over x, y, z_hi), tp: 4 (over z_lo, core).
Axes of the slice: x: 4, y: 4, z: 4 (z_hi: 2, z_lo: 2; z = z_hi * 2 + z_lo), core: 2. Of those that a mesh axis runs over, the one named last changes fastest.
Arguments:
- tokens: bfloat16 [32, 1024, 1024], P('fsdp', 'tp'), may hold values from -6 to 6
- attention_gain: bfloat16 [1024], P('fsdp'), may hold values from 0.25 to 1.75
- query_weight: bfloat16 [1024, 2048], P('fsdp', 'tp'), may hold values from -0.1875 to 0.1875
- key_weight: bfloat16 [1024, 1024], P('fsdp', 'tp'), may hold values from -0.1875 to 0.1875
- value_weight: bfloat16 [1024, 1024], P('fsdp', 'tp'), may hold values from -0.1875 to 0.1875
- query_gain: bfloat16 [128], P('fsdp'), may hold values from 0.25 to 1.75
- key_gain: bfloat16 [128], P('fsdp'), may hold values from 0.25 to 1.75
- output_weight: bfloat16 [1024, 2048], P('fsdp', 'tp'), may hold values from -0.375 to 0.375
- feed_gain: bfloat16 [1024], P('fsdp'), may hold values from 0.25 to 1.75
- gate_weight: bfloat16 [1024, 3072], P('fsdp', 'tp'), may hold values from -0.1875 to 0.1875
- up_weight: bfloat16 [1024, 3072], P('fsdp', 'tp'), may hold values from -0.1875 to 0.1875
- down_weight: bfloat16 [1024, 3072], P('fsdp', 'tp'), may hold values from -0.109375 to 0.109375
- cotangent: bfloat16 [32, 1024, 1024], P('fsdp', 'tp'), may hold values from -6 to 6
Outputs:
- layer_output: bfloat16 [32, 1024, 1024], P('fsdp', 'tp')
- tokens_grad: float32 [32, 1024, 1024], P('fsdp', 'tp')
- attention_gain_grad: float32 [1024], P('fsdp')
- query_weight_grad: float32 [1024, 2048], P('fsdp', 'tp')
- key_weight_grad: float32 [1024, 1024], P('fsdp', 'tp')
- value_weight_grad: float32 [1024, 1024], P('fsdp', 'tp')
- query_gain_grad: float32 [128], P('fsdp')
- key_gain_grad: float32 [128], P('fsdp')
- output_weight_grad: float32 [1024, 2048], P('fsdp', 'tp')
- feed_gain_grad: float32 [1024], P('fsdp')
- gate_weight_grad: float32 [1024, 3072], P('fsdp', 'tp')
- up_weight_grad: float32 [1024, 3072], P('fsdp', 'tp')
- down_weight_grad: float32 [1024, 3072], P('fsdp', 'tp')
All inputs are finite; a program needn't handle non-finite values.
Results may differ from a plain program's by a relative error of at most 0.017.
Values may be sent and summed in bfloat16 or wider, within the bound.
No kernel may reach another device: no remote copies, remote signals or barrier semaphores. Data moves between devices by JAX's collectives and lax.ppermute only.
A program may use at most 192 MiB of HBM per device.

v0:
```python
import math

import jax
import jax.numpy as jnp
from jax import lax
from jax.sharding import PartitionSpec as P

HD = 128
QBLOCK = 512


epsilon = 1e-06
rope_base = 1000000.0
masked_score = -1e30


def sent_together(arrays, axis, dim, along):
    widths = [math.prod(a.shape[along:]) for a in arrays]
    both = jnp.concatenate(
        [a.reshape(*a.shape[:along], w) for a, w in zip(arrays, widths)], axis=along
    )
    whole = lax.all_gather(both, axis, axis=dim, tiled=True)
    parts = jnp.split(whole, [sum(widths[:k]) for k in range(1, len(widths))], axis=along)
    return tuple((b.reshape(*whole.shape[:along], *a.shape[along:]) for a, b in zip(arrays, parts)))


def from_everyone(shard, axis):
    copies = jnp.broadcast_to(shard, (lax.axis_size(axis), *shard.shape))
    return lax.all_to_all(copies, axis, split_axis=0, concat_axis=0, tiled=True)


def in_order(parts, dim):
    parts = jnp.moveaxis(parts, 0, dim)
    shape = parts.shape
    return parts.reshape(*shape[:dim], shape[dim] * shape[dim + 1], *shape[dim + 2 :])


def gather_directly(shard, axis, dim):
    parts = from_everyone(shard, axis)
    return in_order(parts, dim)


def in_blocks(shard, dim, length):
    before, after = (shard.shape[:dim], shard.shape[dim + 1 :])
    return jnp.moveaxis(shard.reshape(*before, length, -1, *after), dim, 0)


def sent_and_summed(shard, axis, dim):
    length = lax.axis_size(axis)
    parts = lax.all_to_all(in_blocks(shard, dim, length), axis, 0, 0, tiled=True)
    return jnp.sum(parts, axis=0)


def side_by_side(arrays, axis, dim, along):
    columns = [a.reshape(*a.shape[:along], -1) for a in arrays]
    both = jnp.concatenate(columns, axis=along)
    whole, at, done = (lax.psum_scatter(both, axis, scatter_dimension=dim, tiled=True), 0, [])
    for a, column in zip(arrays, columns):
        share = whole[..., at : at + column.shape[along]]
        done.append(share.reshape(*share.shape[:along], *a.shape[along:]))
        at += column.shape[along]
    return tuple(done)


def sum_together(arrays, axis, dims):
    length = lax.axis_size(axis)
    parts = [in_blocks(a, dim, length) for a, dim in zip(arrays, dims)]
    lines = jnp.concatenate([b.reshape(length, -1) for b in parts], axis=1)
    rows = max(16, -(-lines.shape[1] // 1024) * 8)
    lines = jnp.pad(lines, ((0, 0), (0, rows * 128 - lines.shape[1]))).reshape(-1, 128)
    line, at, done = (lax.psum_scatter(lines, axis, tiled=True).reshape(-1), 0, [])
    for b in parts:
        part = b[0]
        done.append(line[at : at + part.size].reshape(part.shape))
        at += part.size
    return tuple(done)


def over_copies(shard, axis):
    everything = from_everyone(shard, axis)
    return jnp.sum(everything, axis=0)


def rms_scale(values, gain_vector):
    inverse = lax.rsqrt(jnp.mean(values * values, axis=-1, keepdims=True) + epsilon)
    return values * inverse * gain_vector


def rms_back(values, gain_vector, upstream):
    inverse = lax.rsqrt(jnp.mean(values * values, axis=-1, keepdims=True) + epsilon)
    scaled = gain_vector * upstream
    moment = jnp.mean(scaled * values, axis=-1, keepdims=True)
    grad_values = inverse * scaled - values * (inverse * inverse * inverse) * moment
    gain_terms = (upstream * values * inverse).reshape(-1, values.shape[-1])
    return (grad_values, jnp.sum(gain_terms, axis=0))


def rotary_tables(length, head_size):
    midway = head_size // 2
    frequency = 1.0 / rope_base ** (jnp.arange(midway, dtype=jnp.float32) * 2.0 / head_size)
    angles = jnp.arange(length, dtype=jnp.float32)[:, None] * frequency[None, :]
    cosine_table = jnp.concatenate([jnp.cos(angles), jnp.cos(angles)], axis=1)[:, None, :]
    sine_table = jnp.concatenate([jnp.sin(angles), jnp.sin(angles)], axis=1)[:, None, :]
    return (cosine_table, sine_table)


def rotate(values, cosine_table, sine_table):
    midway = values.shape[-1] // 2
    turned = jnp.concatenate([-values[..., midway:], values[..., :midway]], axis=-1)
    return values * cosine_table + turned * sine_table


def rotate_back(upstream, cosine_table, sine_table):
    midway = upstream.shape[-1] // 2
    product = upstream * sine_table
    turned = jnp.concatenate([product[..., midway:], -product[..., :midway]], axis=-1)
    return upstream * cosine_table + turned


def block_scores(query_block, key_rows, offset, score_scale):
    scores = (
        jnp.einsum("qhgd,khd->hgqk", query_block, key_rows, preferred_element_type=jnp.float32)
        * score_scale
    )
    query_positions = offset + jnp.arange(query_block.shape[0])
    allowed = jnp.arange(key_rows.shape[0])[None, :] <= query_positions[:, None]
    return jnp.where(allowed, scores, masked_score)


def attend_forward(queries, key_rows, value_rows, score_scale):
    length = key_rows.shape[0]
    outputs = []
    log_list = []
    for block_index in range(length // QBLOCK):
        offset = block_index * QBLOCK
        scores = block_scores(queries[offset : offset + QBLOCK], key_rows, offset, score_scale)
        log_total = jax.nn.logsumexp(scores, axis=-1, keepdims=True)
        weights_low = jnp.exp(scores - log_total).astype(jnp.bfloat16)
        outputs.append(
            jnp.einsum(
                "hgqk,khd->qhgd", weights_low, value_rows, preferred_element_type=jnp.float32
            )
        )
        log_list.append(log_total)
    return (jnp.concatenate(outputs, axis=0), jnp.concatenate(log_list, axis=2))


def attend_backward(queries, key_rows, value_rows, grad_out, log_totals, score_scale):
    length = key_rows.shape[0]
    query_list = []
    grad_keys = jnp.zeros(key_rows.shape, jnp.float32)
    grad_values = jnp.zeros(value_rows.shape, jnp.float32)
    for block_index in range(length // QBLOCK):
        offset = block_index * QBLOCK
        query_block = queries[offset : offset + QBLOCK]
        grad_block = grad_out[offset : offset + QBLOCK]
        scores = block_scores(query_block, key_rows, offset, score_scale)
        probabilities = jnp.exp(scores - log_totals[:, :, offset : offset + QBLOCK])
        weights_low = probabilities.astype(jnp.bfloat16)
        grad_probs = jnp.einsum(
            "qhgd,khd->hgqk", grad_block, value_rows, preferred_element_type=jnp.float32
        )
        row_dot = jnp.sum(probabilities * grad_probs, axis=-1, keepdims=True)
        grad_scores = (probabilities * (grad_probs - row_dot)).astype(jnp.bfloat16)
        query_list.append(
            jnp.einsum("hgqk,khd->qhgd", grad_scores, key_rows, preferred_element_type=jnp.float32)
            * score_scale
        )
        grad_keys = (
            grad_keys
            + jnp.einsum(
                "hgqk,qhgd->khd", grad_scores, query_block, preferred_element_type=jnp.float32
            )
            * score_scale
        )
        grad_values = grad_values + jnp.einsum(
            "hgqk,qhgd->khd", weights_low, grad_block, preferred_element_type=jnp.float32
        )
    return (jnp.concatenate(query_list, axis=0), grad_keys, grad_values)


def local(
    tokens,
    attention_gain,
    query_weight,
    key_weight,
    value_weight,
    query_gain,
    key_gain,
    output_weight,
    feed_gain,
    gate_weight,
    up_weight,
    down_weight,
    cotangent,
):
    sequences, share_rows, model_width = tokens.shape
    length = share_rows * lax.axis_size("tp")
    row_count = sequences * length
    local_heads = query_weight.shape[1] // HD
    local_groups = key_weight.shape[1] // HD
    group_size = local_heads // local_groups
    score_scale = 1.0 / math.sqrt(HD)
    cosine_table, sine_table = rotary_tables(length, HD)
    attention_set = (
        *sent_together((attention_gain, query_weight, key_weight, value_weight), "fsdp", 0, 1),
        lax.all_gather(query_gain, "fsdp", axis=0, tiled=True),
        lax.all_gather(key_gain, "fsdp", axis=0, tiled=True),
        lax.all_gather(output_weight, "fsdp", axis=0, tiled=True),
    )
    stream = tokens.astype(jnp.float32)
    first_low = rms_scale(stream, attention_set[0]).astype(jnp.bfloat16)
    first_full = gather_directly(first_low, "tp", 1).reshape(row_count, model_width)
    queries_raw = jnp.dot(first_full, attention_set[1], preferred_element_type=jnp.float32).reshape(
        sequences, length, local_heads, HD
    )
    keys_raw = jnp.dot(first_full, attention_set[2], preferred_element_type=jnp.float32).reshape(
        sequences, length, local_groups, HD
    )
    values_low = (
        jnp.dot(first_full, attention_set[3], preferred_element_type=jnp.float32)
        .astype(jnp.bfloat16)
        .reshape(sequences, length, local_groups, HD)
    )
    queries_low = (
        rotate(rms_scale(queries_raw, attention_set[4]), cosine_table, sine_table)
        .astype(jnp.bfloat16)
        .reshape(sequences, length, local_groups, group_size, HD)
    )
    keys_low = rotate(rms_scale(keys_raw, attention_set[5]), cosine_table, sine_table).astype(
        jnp.bfloat16
    )
    attended, log_totals = lax.map(
        lambda element: attend_forward(element[0], element[1], element[2], score_scale),
        (queries_low, keys_low, values_low),
    )
    attended_low = attended.astype(jnp.bfloat16).reshape(row_count, local_heads * HD)
    branch_part = jnp.einsum(
        "rc,dc->rd", attended_low, attention_set[6], preferred_element_type=jnp.float32
    ).reshape(sequences, length, model_width)
    middle = stream + sent_and_summed(branch_part, "tp", 1)
    feed_set = sent_together((feed_gain, gate_weight, up_weight, down_weight), "fsdp", 0, 1)
    second_low = rms_scale(middle, feed_set[0]).astype(jnp.bfloat16)
    second_full = gather_directly(second_low, "tp", 1).reshape(row_count, model_width)
    gate_values = jnp.dot(second_full, feed_set[1], preferred_element_type=jnp.float32)
    up_values = jnp.dot(second_full, feed_set[2], preferred_element_type=jnp.float32)
    sigmoid_gate = jax.nn.sigmoid(gate_values)
    hidden_low = (gate_values * sigmoid_gate * up_values).astype(jnp.bfloat16)
    feed_part = jnp.einsum(
        "rf,df->rd", hidden_low, feed_set[3], preferred_element_type=jnp.float32
    ).reshape(sequences, length, model_width)
    layer_output = (middle + sent_and_summed(feed_part, "tp", 1)).astype(jnp.bfloat16)
    feed_back = sent_together((feed_gain, gate_weight, up_weight, down_weight), "fsdp", 0, 1)
    grad_full = gather_directly(cotangent, "tp", 1).reshape(row_count, model_width)
    grad_hidden = jnp.dot(grad_full, feed_back[3], preferred_element_type=jnp.float32)
    down_grad = jnp.einsum("rd,rf->df", grad_full, hidden_low, preferred_element_type=jnp.float32)
    grad_gate = (
        grad_hidden * up_values * sigmoid_gate * (1.0 + gate_values * (1.0 - sigmoid_gate))
    ).astype(jnp.bfloat16)
    grad_up = (grad_hidden * gate_values * sigmoid_gate).astype(jnp.bfloat16)
    gate_grad = jnp.einsum("rd,rf->df", second_full, grad_gate, preferred_element_type=jnp.float32)
    up_grad = jnp.einsum("rd,rf->df", second_full, grad_up, preferred_element_type=jnp.float32)
    grad_second_part = jnp.einsum(
        "rf,df->rd", grad_gate, feed_back[1], preferred_element_type=jnp.float32
    )
    grad_second_part = grad_second_part + jnp.einsum(
        "rf,df->rd", grad_up, feed_back[2], preferred_element_type=jnp.float32
    )
    grad_second = sent_and_summed(grad_second_part.reshape(sequences, length, model_width), "tp", 1)
    grad_norm, feed_gain_part = rms_back(middle, feed_back[0], grad_second)
    grad_middle = cotangent.astype(jnp.float32) + grad_norm
    feed_summed = side_by_side((feed_gain_part, gate_grad, up_grad, down_grad), "fsdp", 0, 1)
    branch_full = gather_directly(grad_middle.astype(jnp.bfloat16), "tp", 1).reshape(
        row_count, model_width
    )
    attention_back = (
        *sent_together((attention_gain, query_weight, key_weight, value_weight), "fsdp", 0, 1),
        lax.all_gather(query_gain, "fsdp", axis=0, tiled=True),
        lax.all_gather(key_gain, "fsdp", axis=0, tiled=True),
        lax.all_gather(output_weight, "fsdp", axis=0, tiled=True),
    )
    grad_attended = jnp.dot(
        branch_full, attention_back[6], preferred_element_type=jnp.float32
    ).astype(jnp.bfloat16)
    output_grad = jnp.einsum(
        "rd,rc->dc", branch_full, attended_low, preferred_element_type=jnp.float32
    )
    grad_attended = grad_attended.reshape(sequences, length, local_groups, group_size, HD)
    grad_query_rot, grad_key_rot, grad_values = lax.map(
        lambda element: attend_backward(
            element[0], element[1], element[2], element[3], element[4], score_scale
        ),
        (queries_low, keys_low, values_low, grad_attended, log_totals),
    )
    grad_query_norm = rotate_back(
        grad_query_rot.reshape(sequences, length, local_heads, HD), cosine_table, sine_table
    )
    grad_queries, query_gain_part = rms_back(queries_raw, attention_back[4], grad_query_norm)
    grad_keys, key_gain_part = rms_back(
        keys_raw, attention_back[5], rotate_back(grad_key_rot, cosine_table, sine_table)
    )
    queries_grad_low = grad_queries.astype(jnp.bfloat16).reshape(row_count, local_heads * HD)
    keys_grad_low = grad_keys.astype(jnp.bfloat16).reshape(row_count, local_groups * HD)
    values_grad_low = grad_values.astype(jnp.bfloat16).reshape(row_count, local_groups * HD)
    query_grad = jnp.einsum(
        "rd,rc->dc", first_full, queries_grad_low, preferred_element_type=jnp.float32
    )
    key_grad = jnp.einsum(
        "rd,rc->dc", first_full, keys_grad_low, preferred_element_type=jnp.float32
    )
    value_grad = jnp.einsum(
        "rd,rc->dc", first_full, values_grad_low, preferred_element_type=jnp.float32
    )
    grad_first_part = jnp.einsum(
        "rc,dc->rd", queries_grad_low, attention_back[1], preferred_element_type=jnp.float32
    )
    grad_first_part = grad_first_part + jnp.einsum(
        "rc,dc->rd", keys_grad_low, attention_back[2], preferred_element_type=jnp.float32
    )
    grad_first_part = grad_first_part + jnp.einsum(
        "rc,dc->rd", values_grad_low, attention_back[3], preferred_element_type=jnp.float32
    )
    grad_first = sent_and_summed(grad_first_part.reshape(sequences, length, model_width), "tp", 1)
    grad_stream, attention_gain_part = rms_back(stream, attention_back[0], grad_first)
    tokens_grad = grad_middle + grad_stream
    attention_summed = sum_together(
        (
            attention_gain_part,
            query_grad,
            key_grad,
            value_grad,
            query_gain_part,
            key_gain_part,
            output_grad,
        ),
        "fsdp",
        (0, 0, 0, 0, 0, 0, 0),
    )
    summed = attention_summed + feed_summed
    gain_totals = (
        over_copies(summed[0], "tp"),
        over_copies(summed[4], "tp"),
        over_copies(summed[5], "tp"),
        over_copies(summed[7], "tp"),
    )
    return (
        layer_output,
        tokens_grad,
        gain_totals[0],
        summed[1],
        summed[2],
        summed[3],
        gain_totals[1],
        gain_totals[2],
        summed[6],
        gain_totals[3],
        summed[8],
        summed[9],
        summed[10],
    )


def solution(mesh):
    placed = (
        P("fsdp", "tp", None),
        P("fsdp"),
        P("fsdp", "tp"),
        P("fsdp", "tp"),
        P("fsdp", "tp"),
        P("fsdp"),
        P("fsdp"),
        P("fsdp", "tp"),
        P("fsdp"),
        P("fsdp", "tp"),
        P("fsdp", "tp"),
        P("fsdp", "tp"),
        P("fsdp", "tp", None),
    )
    return jax.shard_map(
        local,
        mesh=mesh,
        in_specs=placed,
        out_specs=(
            P("fsdp", "tp", None),
            P("fsdp", "tp", None),
            P("fsdp"),
            P("fsdp", "tp"),
            P("fsdp", "tp"),
            P("fsdp", "tp"),
            P("fsdp"),
            P("fsdp"),
            P("fsdp", "tp"),
            P("fsdp"),
            P("fsdp", "tp"),
            P("fsdp", "tp"),
            P("fsdp", "tp"),
        ),
        check_vma=False,
    )
```

profile of v0, /device:TPU:28, one launch (start us, length us, event | category | flops | bytes accessed | tf_op | source)
XLA Modules:
  0.0 1125.2 jit_solution(17822053571279785839)
XLA Ops:
  12.1 72.7 %all-gather.4.cloned.1.call-done = bf16[1024,1025]{1,0:T(8,128)(2,1)} async-done(((bf16[32,1025]{1,0:T(8,128)(2,1)}), bf16[1024,1025]{1,0:T(8,128)(2,1)}) %all-gather.4.cloned.1.call-update) | async-done | bytes 2099216 | tf_op jit(solution)/shard_map/all_gather | solution.py:22
  95.3 93.0 %all-reduce.4 = (bf16[128]{0:T(256)(128)(2,1)S(1)}, bf16[128]{0:T(256)(128)(2,1)S(1)}) all-reduce(bf16[128]{0:T(256)(128)(2,1)S(1)} %dynamic-update-slice, bf16[128]{0:T(256)(128)(2,1)S(1)} %dynamic-update-slice.1), channel_id=1, replica_groups=mesh['fsdp'=32,'tp'=4] {'fsdp'}, use_global_device_ids=true, to_apply=%add.1 | all-reduce | flops 256 | bytes 1024
  236.0 51.7 %all_to_all.64 = f32[4,1,256,1024]{3,2,1,0:T(8,128)} all-to-all(f32[4,1,256,1024]{3,2,1,0:T(8,128)S(1)} %convolution_bitcast_fusion), channel_id=1, replica_groups=mesh['fsdp'=32,'tp'=4] {'tp'}, dimensions={0} | all-to-all | bytes 8388608 | tf_op jit(solution)/shard_map/all_to_all | solution.py:50
  303.2 16.3 %all-to-all-done.4 = bf16[4,1,256,1024]{3,2,1,0:T(8,128)(2,1)} async-done(((bf16[4,1,256,1024]{3,2,1,0:T(8,128)(2,1)}), bf16[4,1,256,1024]{3,2,1,0:T(8,128)(2,1)}, u32[]{:S(2)}, u32[]{:S(2)}) %all-to-all-start.4) | async-done | bytes 2097184 | tf_op jit(solution)/shard_map/all_to_all | solution.py:29
  326.8 5.7 fusion.28
  332.5 20.0 %all-to-all-done.2 = bf16[4,1,256,1024]{3,2,1,0:T(8,128)(2,1)} async-done(((bf16[4,1,256,1024]{3,2,1,0:T(8,128)(2,1)}), bf16[4,1,256,1024]{3,2,1,0:T(8,128)(2,1)}, u32[]{:S(2)}, u32[]{:S(2)}) %all-to-all-start.2) | async-done | bytes 2097184 | tf_op jit(solution)/shard_map/all_to_all | solution.py:29
  356.7 6.7 fusion.14
  374.1 6.0 fusion.30
  380.1 42.2 %all-to-all-done.5 = f32[4,1,256,1024]{3,2,1,0:T(8,128)} async-done(((f32[4,1,256,1024]{3,2,1,0:T(8,128)}), f32[4,1,256,1024]{3,2,1,0:T(8,128)}, u32[]{:S(2)}, u32[]{:S(2)}) %all-to-all-start.5) | async-done | bytes 4194336 | tf_op jit(solution)/shard_map/all_to_all | solution.py:50
  422.4 5.1 all-to-all-start.3
  433.0 42.7 %all-to-all-done.3 = f32[4,1,256,1024]{3,2,1,0:T(8,128)} async-done(((f32[4,1,256,1024]{3,2,1,0:T(8,128)}), f32[4,1,256,1024]{3,2,1,0:T(8,128)}, u32[]{:S(2)}, u32[]{:S(2)}) %all-to-all-start.3) | async-done | bytes 4194336 | tf_op jit(solution)/shard_map/all_to_all | solution.py:50
  489.0 25.7 %all-to-all-done.6 = bf16[4,1,256,1024]{3,2,1,0:T(8,128)(2,1)} async-done(((bf16[4,1,256,1024]{3,2,1,0:T(8,128)(2,1)}), bf16[4,1,256,1024]{3,2,1,0:T(8,128)(2,1)}, u32[]{:S(2)}, u32[]{:S(2)}) %all-to-all-start.6) | async-done | bytes 2097184 | tf_op jit(solution)/shard_map/all_to_all | solution.py:29
  518.1 6.0 convolution_bitcast_fusion.2
  524.1 5.1 fusion
  529.3 5.2 fusion.2
  577.3 4.9 all-to-all-start.7
  623.0 7.4 all-to-all-done.7
  635.1 9.3 dynamic-update-slice.3
  644.4 6.3 dynamic-update-slice.4
  650.7 6.6 dynamic-update-slice.5
  660.4 8.8 dynamic-update-slice.8
  669.2 5.9 pad.4
  675.1 6.3 reshape.771
  681.5 5.6 fusion.95
  687.1 5.3 fusion.96
  692.4 5.2 convolution_bitcast_fusion.1
  697.6 28.3 %concatenate.108 = f32[1024,2305]{0,1:T(8,128)} concatenate(f32[1024,1]{0,1:T(1,128)S(1)} %bitcast.342, f32[1024,768]{0,1:T(8,128)} %fusion.95, f32[1024,768]{0,1:T(8,128)} %fusion.96, f32[1024,768]{0,1:T(8,128)} %convolution_bitcast_fusion.1), dimensions={1} | concatenate | bytes 18882560 | tf_op jit(solution)/shard_map/concatenate | solution.py:56
  725.9 10.5 copy.384
  738.9 137.1 %reduce-scatter.10.cloned.1.call-done = f32[392,128]{1,0:T(8,128)} async-done(((f32[12544,128]{1,0:T(8,128)}), f32[392,128]{1,0:T(8,128)}) %reduce-scatter.10.cloned.1.call-update) | async-done | bytes 200720
  880.8 6.1 all_to_all.65
  886.8 6.1 all_to_all.66
  902.7 206.6 %reduce-scatter.8.cloned.1.call-done = f32[32,2305]{1,0:T(8,128)} async-done(((f32[1024,2305]{1,0:T(8,128)}), f32[32,2305]{1,0:T(8,128)}) %reduce-scatter.8.cloned.1.call-update) | async-done | bytes 295056
  (300 shorter events, 238.5 us)
Async XLA Ops:
  7.2 77.6 %all-gather.4.cloned.1.call-start = ((), (), s32[]{:S(2)}) async-start(), calls=%async_computation.14 | async-start | bytes 2433024 | tf_op jit(solution)/shard_map/all_gather | solution.py:22
  9.5 223.6 %all-gather.6.cloned.1.call-start = ((), (), s32[]{:S(2)}) async-start(), calls=%async_computation.15 | async-start | bytes 1081344 | tf_op jit(solution)/shard_map/all_gather | solution.py:209
  12.1 76.7 %copy-start.50 = (f32[256]{0:T(256)}, f32[256]{0:T(256)S(1)}, u32[]{:S(2)}) copy-start(f32[256]{0:T(256)S(1)} %get-tuple-element.207) | copy-start | bytes 3076
  88.8 6.1 copy-start.54
  88.8 6.3 copy-start.55
  88.8 106.2 %all-to-all-start = ((bf16[4,1,256,1024]{3,2,1,0:T(8,128)(2,1)}), bf16[4,1,256,1024]{3,2,1,0:T(8,128)(2,1)S(1)}, u32[]{:S(2)}, u32[]{:S(2)}) async-start(bf16[4,1,256,1024]{3,2,1,0:T(8,128)(2,1)} %broadcast_in_dim.110), calls=%async_computation | async-start | bytes 4194304 | tf_op jit(solution)/shard_map/all_to_all | solution.py:29
  92.6 207.3 %all-gather.8.cloned.1.call-start = ((), (), s32[]{:S(2)}) async-start(), calls=%async_computation.16 | async-start | bytes 5136384 | tf_op jit(solution)/shard_map/all_gather | solution.py:22
  190.7 8.6 copy-start.14
  190.7 8.6 copy-start.23
  215.3 8.6 copy-start.1
  217.5 8.8 copy-start
  236.0 51.7 %copy-start.36 = (bf16[1,256,1024]{2,1,0:T(8,128)(2,1)S(1)}, bf16[1,256,1024]{2,1,0:T(8,128)(2,1)}, u32[]{:S(2)}) copy-start(bf16[1,256,1024]{2,1,0:T(8,128)(2,1)} %param.25) | copy-start | bytes 1572868
  289.2 30.2 %all-to-all-start.4 = ((bf16[4,1,256,1024]{3,2,1,0:T(8,128)(2,1)}), bf16[4,1,256,1024]{3,2,1,0:T(8,128)(2,1)}, u32[]{:S(2)}, u32[]{:S(2)}) async-start(bf16[4,1,256,1024]{3,2,1,0:T(8,128)(2,1)} %broadcast_in_dim.115), calls=%async_computation.4 | async-start | bytes 4194304 | tf_op jit(solution)/shard_map/all_to_all | solution.py:29
  322.2 30.3 %all-to-all-start.2 = ((bf16[4,1,256,1024]{3,2,1,0:T(8,128)(2,1)}), bf16[4,1,256,1024]{3,2,1,0:T(8,128)(2,1)}, u32[]{:S(2)}, u32[]{:S(2)}) async-start(bf16[4,1,256,1024]{3,2,1,0:T(8,128)(2,1)} %broadcast_in_dim.114), calls=%async_computation.2 | async-start | bytes 4194304 | tf_op jit(solution)/shard_map/all_to_all | solution.py:29
  352.5 10.9 slice-start.4
  356.7 6.7 slice-start.5
  369.3 53.1 %all-to-all-start.5 = ((f32[4,1,256,1024]{3,2,1,0:T(8,128)}), f32[4,1,256,1024]{3,2,1,0:T(8,128)}, u32[]{:S(2)}, u32[]{:S(2)}) async-start(f32[4,1,256,1024]{3,2,1,0:T(8,128)} %bitcast.321), calls=%async_computation.5 | async-start | bytes 8388608 | tf_op jit(solution)/shard_map/all_to_all | solution.py:50
  422.4 53.3 %all-to-all-start.3 = ((f32[4,1,256,1024]{3,2,1,0:T(8,128)}), f32[4,1,256,1024]{3,2,1,0:T(8,128)}, u32[]{:S(2)}, u32[]{:S(2)}) async-start(f32[4,1,256,1024]{3,2,1,0:T(8,128)} %bitcast.320), calls=%async_computation.3 | async-start | bytes 8388608 | tf_op jit(solution)/shard_map/all_to_all | solution.py:50
  484.5 30.2 %all-to-all-start.6 = ((bf16[4,1,256,1024]{3,2,1,0:T(8,128)(2,1)}), bf16[4,1,256,1024]{3,2,1,0:T(8,128)(2,1)}, u32[]{:S(2)}, u32[]{:S(2)}) async-start(bf16[4,1,256,1024]{3,2,1,0:T(8,128)(2,1)} %broadcast_in_dim.116), calls=%async_computation.6 | async-start | bytes 4194304 | tf_op jit(solution)/shard_map/all_to_all | solution.py:29
  514.7 9.4 slice-start.2
  518.1 6.0 slice-start.3
  529.3 7.5 slice-start
  529.3 7.5 slice-start.1
  577.3 53.1 %all-to-all-start.7 = ((f32[4,1,256,1024]{3,2,1,0:T(8,128)}), f32[4,1,256,1024]{3,2,1,0:T(8,128)}, u32[]{:S(2)}, u32[]{:S(2)}) async-start(f32[4,1,256,1024]{3,2,1,0:T(8,128)} %bitcast.309), calls=%async_computation.7 | async-start | bytes 8388608 | tf_op jit(solution)/shard_map/all_to_all | solution.py:50
  582.2 293.9 %reduce-scatter.10.cloned.1.call-start = ((), (), s32[]{:S(2)}) async-start(), calls=%async_computation.18 | async-start | bytes 6623232
  623.0 10.2 copy-start.13
  623.0 10.2 copy-start.46
  623.0 10.2 copy-start.51
  633.6 10.8 copy-start.34
  681.4 427.9 %reduce-scatter.8.cloned.1.call-start = ((), (), s32[]{:S(2)}) async-start(), calls=%async_computation.17 | async-start | bytes 10272768
  893.5 8.7 all-to-all-start.8
  1110.8 6.9 all-to-all-start.11
  (49 other events, 142.4 us)
Sparse Core Ops, SparseCore 0:
  11.5 73.2 all-gather.3
  87.8 64.1 all-gather.5
  155.5 83.3 all-gather.7
  681.6 194.4 reduce-scatter.9
  878.3 231.0 reduce-scatter.7
where the time goes:
time: 1140 us; the launch traced here: 1130 us
  waiting for transfers between devices  577 us (51%)
  local copies, waits for them, and re-layouts  160 us (14%)
  blocking collectives  157 us (14%)
  matrix products  105 us (9%)
  other arithmetic  72 us (6%)
  starting transfers between devices  38.6 us (3%)
  between operations  16.1 us (1%)
    unnamed x7, waiting for transfers between devices  345 us
    unnamed x1, blocking collectives  93 us
    all_to_all x3, waiting for transfers between devices, sent_and_summed(): lax.all_to_all(in_blocks(shard, dim, length), axis, 0, 0, tiled=True)  92.3 us
    all_gather x2, waiting for transfers between devices, sent_together(): whole = lax.all_gather(both, axis, axis=dim, tiled=True)  72.7 us
    all_to_all x6, waiting for transfers between devices, from_everyone(): return lax.all_to_all(copies, axis, split_axis=0, concat_axis=0, tiled=True)  67.1 us
    all_to_all x1, blocking collectives, sent_and_summed(): lax.all_to_all(in_blocks(shard, dim, length), axis, 0, 0, tiled=True)  51.7 us
    unnamed x147, local copies, waits for them, and re-layouts  49.8 us
    concatenate x1, local copies, waits for them, and re-layouts, side_by_side(): both = jnp.concatenate(columns, axis=along)  28.3 us
  transfers between devices with their start and end apart: 14, of which 11 were waited for; matrix products, arithmetic and copies ran while one was open for 16% of the time, Pallas kernels for 0%

commit v1 on v0

v1 whole, which is shorter than its diff:
```python
import math

import jax
import jax.numpy as jnp
from jax import lax
from jax.experimental import pallas as pl
from jax.experimental.pallas import tpu as pltpu
from jax.sharding import Mesh, PartitionSpec as P

HD = 128
ROWS = 256
GROUP = 2
epsilon = 1e-06
rope_base = 1000000.0
score_scale = 1.0 / math.sqrt(HD)
log2_scale = score_scale / math.log(2.0)
FSDP = ("x", "y", "zh")
EVERY = ("x", "y", "zh", "zl", "core")
f32 = jnp.float32
bf16 = jnp.bfloat16


def matmul(a, b):
    return lax.dot_general(a, b, (((1,), (0,)), ((), ())), preferred_element_type=f32)


def matmul_t(a, b):
    return lax.dot_general(a, b, (((1,), (1,)), ((), ())), preferred_element_type=f32)


def t_matmul(a, b):
    return lax.dot_general(a, b, (((0,), (0,)), ((), ())), preferred_element_type=f32)


def inverse_rms(values):
    return lax.rsqrt(jnp.mean(values * values, axis=-1, keepdims=True) + epsilon)


def norm_back(values, gain, upstream):
    inverse = inverse_rms(values)
    scaled = gain * upstream
    moment = jnp.mean(scaled * values, axis=-1, keepdims=True)
    grad = inverse * scaled - values * (inverse * inverse * inverse) * moment
    return grad, jnp.sum(upstream * values * inverse, axis=0, keepdims=True)


def params(**kw):
    return pltpu.CompilerParams(vmem_limit_bytes=56 * 1024 * 1024, **kw)


def cost(flops, nbytes, trans=0):
    return pl.CostEstimate(flops=int(flops), bytes_accessed=int(nbytes), transcendentals=int(trans))


def whole(shape, index=None):
    index = index or (0,) * len(shape)
    return pl.BlockSpec(shape, lambda i, *_: index)


def pick(which, pieces, target):
    for k, piece in enumerate(pieces):

        @pl.when(which == k)
        def _(piece=piece):
            target[...] = piece[...]


def forward_attention_kernel(place, *refs):
    tokens = refs[:4]
    gain, qgain, kgain, wqkv, wo, cos, sin = refs[4:11]
    first, qraw, kraw, low, att, totals, part = refs[11:18]
    rows, keys, values, acc = refs[18:]
    i = pl.program_id(0)
    pick(place[i], tokens, rows)
    x = rows[...].astype(f32)
    normed = (x * inverse_rms(x) * gain[...]).astype(bf16)
    first[...] = normed
    qkv = matmul(normed, wqkv[...])
    nq = qraw.shape[1]
    nk = kraw.shape[1]
    qraw[...] = qkv[:, :nq]
    kraw[...] = qkv[:, nq : nq + nk]
    here = pl.ds(i * ROWS, ROWS)
    c, s = cos[...], sin[...]

    def turned(v, g):
        n = v * inverse_rms(v) * g
        return (n * c + pltpu.roll(n, HD // 2, 1) * s).astype(bf16)

    for h in range(nk // HD):
        k_low = turned(qkv[:, nq + h * HD : nq + (h + 1) * HD], kgain[...])
        v_low = qkv[:, nq + nk + h * HD : nq + nk + (h + 1) * HD].astype(bf16)
        low[:, nq + h * HD : nq + (h + 1) * HD] = k_low
        low[:, nq + nk + h * HD : nq + nk + (h + 1) * HD] = v_low
        keys[h, here, :] = k_low
        values[h, here, :HD] = v_low
        values[h, here, HD:] = jnp.ones((ROWS, HD), bf16)
    mask_q = lax.broadcasted_iota(jnp.int32, (GROUP * ROWS, ROWS), 0) % ROWS
    mask_k = lax.broadcasted_iota(jnp.int32, (GROUP * ROWS, ROWS), 1)
    outs = []
    sums = []
    for h in range(nk // HD):
        qs = []
        for a in range(GROUP):
            col = (h * GROUP + a) * HD
            q_low = turned(qkv[:, col : col + HD], qgain[...])
            low[:, col : col + HD] = q_low
            qs.append(q_low)
        q2 = jnp.concatenate(qs, axis=0)
        scores = matmul_t(q2, keys[h, here, :])
        weights = jnp.where(mask_k <= mask_q, jnp.exp2(scores * log2_scale), 0.0)
        acc[...] = matmul(weights.astype(bf16), values[h, here, :])

        def step(j, _, h=h, q2=q2):
            there = pl.ds(pl.multiple_of(j * ROWS, ROWS), ROWS)
            scores = matmul_t(q2, keys[h, there, :])
            weights = jnp.exp2(scores * log2_scale).astype(bf16)
            acc[...] += matmul(weights, values[h, there, :])
            return 0

        lax.fori_loop(0, i, step, 0)
        total = acc[:, HD:]
        o = (acc[:, :HD] / total).astype(bf16)
        outs += [o[a * ROWS : (a + 1) * ROWS] for a in range(GROUP)]
        sums.append(jnp.log2(total).T[:1, :])
    totals[0] = jnp.concatenate(sums + [jnp.zeros((8 - len(sums), GROUP * ROWS), f32)], axis=0)
    together = jnp.concatenate(outs, axis=1)
    att[...] = together
    part[0] = matmul_t(together, wo[...]).astype(bf16)


def forward_attention(place, tokens, gain, qgain, kgain, weights, nq, nk, cos, sin):
    n, width = 4, tokens[0].shape[1]
    length = n * ROWS
    nqkv = nq + 2 * nk
    row = lambda cols: pl.BlockSpec((ROWS, cols), lambda i, p: (i, 0))
    out = [
        ((length, width), bf16, row(width)),
        ((length, nq), f32, row(nq)),
        ((length, nk), f32, row(nk)),
        ((length, nqkv), bf16, row(nqkv)),
        ((length, nq), bf16, row(nq)),
        ((n, 8, GROUP * ROWS), f32, pl.BlockSpec((1, 8, GROUP * ROWS), lambda i, p: (i, 0, 0))),
        ((n, ROWS, width), bf16, pl.BlockSpec((1, ROWS, width), lambda i, p: (p[i], 0, 0))),
    ]
    return pl.pallas_call(
        forward_attention_kernel,
        grid_spec=pltpu.PrefetchScalarGridSpec(
            num_scalar_prefetch=1,
            grid=(n,),
            in_specs=[
                *[whole((ROWS, width))] * 4,
                whole((1, width)),
                whole((1, HD)),
                whole((1, HD)),
                whole((width, nqkv)),
                whole((width, nq), (0, nqkv // nq)),
                row(HD),
                row(HD),
            ],
            out_specs=[o[2] for o in out],
            scratch_shapes=[
                pltpu.VMEM((ROWS, width), bf16),
                pltpu.VMEM((nk // HD, length, HD), bf16),
                pltpu.VMEM((nk // HD, length, 2 * HD), bf16),
                pltpu.VMEM((GROUP * ROWS, 2 * HD), f32),
            ],
        ),
        out_shape=[jax.ShapeDtypeStruct(o[0], o[1]) for o in out],
        compiler_params=params(),
        cost_estimate=cost(7e9, 16e6, 3e6),
        name="forward_attention",
    )(place, *tokens, gain, qgain, kgain, weights, weights, cos, sin)


def middle_kernel(tokens, mine, from_core, from_z, gain, middle, second):
    total = mine[...].astype(f32) + from_core[...].astype(f32) + from_z[...].astype(f32)
    v = tokens[...].astype(f32) + total
    middle[...] = v
    second[...] = (v * inverse_rms(v) * gain[...]).astype(bf16)


def middle_step(tokens, part, from_core, from_z, gain):
    width = tokens.shape[1]
    half = ROWS // 2
    row = pl.BlockSpec((half, width), lambda i: (i, 0))
    first = pl.BlockSpec((None, None, half, width), lambda i: (0, 0, i, 0))
    return pl.pallas_call(
        middle_kernel,
        grid=(2,),
        in_specs=[row, first, pl.BlockSpec((None, half, width), lambda i: (0, i, 0)), row, whole((1, width))],
        out_specs=[row, row],
        out_shape=[jax.ShapeDtypeStruct((ROWS, width), f32), jax.ShapeDtypeStruct((ROWS, width), bf16)],
        compiler_params=params(),
        cost_estimate=cost(2e6, 4e6),
        name="middle_step",
    )(tokens, part, from_core, from_z, gain)


def feed_kernel(*refs):
    second, grads = refs[:4], refs[4:8]
    wg, wu, wd = refs[8:11]
    hidden, grad_units, part = refs[11:14]
    rows_s, rows_g = refs[14:]
    i = pl.program_id(0)
    pick(i, second, rows_s)
    pick(i, grads, rows_g)
    s = rows_s[...]
    gate = matmul(s, wg[...])
    up = matmul(s, wu[...])
    sig = 1.0 / (1.0 + jnp.exp(-gate))
    swish = gate * sig
    hidden[...] = (swish * up).astype(bf16)
    gh = matmul(rows_g[...], wd[...])
    gg = (gh * up * sig * (1.0 + gate * (1.0 - sig))).astype(bf16)
    gu = (gh * swish).astype(bf16)
    units = wg.shape[1]
    grad_units[:, :units] = gg
    grad_units[:, units:] = gu
    part[0] = (matmul_t(gg, wg[...]) + matmul_t(gu, wu[...])).astype(bf16)


def feed_step(second, grads, weights, units):
    width = second[0].shape[1]
    length = 4 * ROWS
    row = lambda cols: pl.BlockSpec((ROWS, cols), lambda i: (i, 0))
    return pl.pallas_call(
        feed_kernel,
        grid=(4,),
        in_specs=[
            *[whole((ROWS, width))] * 8,
            whole((width, units)),
            whole((width, units), (0, 1)),
            whole((width, units), (0, 2)),
        ],
        out_specs=[row(units), row(2 * units), pl.BlockSpec((1, ROWS, width), lambda i: (i, 0, 0))],
        out_shape=[
            jax.ShapeDtypeStruct((length, units), bf16),
            jax.ShapeDtypeStruct((length, 2 * units), bf16),
            jax.ShapeDtypeStruct((4, ROWS, width), bf16),
        ],
        scratch_shapes=[pltpu.VMEM((ROWS, width), bf16)] * 2,
        compiler_params=params(),
        cost_estimate=cost(8e9, 16e6, 1e6),
        name="feed_step",
    )(*second, *grads, weights, weights, weights)


def feed_out_kernel(hidden, wd, part):
    part[0] = matmul_t(hidden[...], wd[...]).astype(bf16)


def feed_out(hidden, weights):
    length, units = hidden.shape
    width = weights.shape[0]
    return pl.pallas_call(
        feed_out_kernel,
        grid=(4,),
        in_specs=[pl.BlockSpec((ROWS, units), lambda i: (i, 0)), whole((width, units), (0, 2))],
        out_specs=pl.BlockSpec((1, ROWS, width), lambda i: (i, 0, 0)),
        out_shape=jax.ShapeDtypeStruct((4, ROWS, width), bf16),
        compiler_params=params(),
        cost_estimate=cost(1.6e9, 5e6),
        name="feed_out",
    )(hidden, weights)


def feed_weights_kernel(*refs):
    second, grads = refs[:4], refs[4:8]
    grad_units, hidden, out = refs[8:]
    wide = grad_units.shape[1]

    def over(pieces, other):
        total = None
        for k, piece in enumerate(pieces):
            term = t_matmul(piece[...], other[k * ROWS : (k + 1) * ROWS, :])
            total = term if total is None else total + term
        return total.astype(bf16)

    out[:, :wide] = over(second, grad_units)
    out[:, wide:] = over(grads, hidden)


def feed_weights(second, grads, grad_units, hidden):
    width = second[0].shape[1]
    length, wide = grad_units.shape
    units = hidden.shape[1]
    return pl.pallas_call(
        feed_weights_kernel,
        grid=(width // 256,),
        in_specs=[
            *[pl.BlockSpec((ROWS, 256), lambda i: (0, i))] * 8,
            whole((length, wide)),
            whole((length, units)),
        ],
        out_specs=pl.BlockSpec((256, wide + units), lambda i: (i, 0)),
        out_shape=jax.ShapeDtypeStruct((width, wide + units), bf16),
        compiler_params=params(),
        cost_estimate=cost(4.8e9, 14e6),
        name="feed_weights",
    )(*second, *grads, grad_units, hidden)


def middle_back_kernel(middle, mine, from_core, from_z, cotangent, gain, grad_middle, branch, gain_part):
    u = mine[...].astype(f32) + from_core[...].astype(f32) + from_z[...].astype(f32)
    grad, part = norm_back(middle[...], gain[...], u)
    grad = cotangent[...].astype(f32) + grad
    grad_middle[...] = grad
    branch[...] = grad.astype(bf16)

    @pl.when(pl.program_id(0) == 0)
    def _():
        gain_part[...] = jnp.zeros_like(gain_part)

    gain_part[:1, :] += part


def middle_back(middle, part, from_core, from_z, cotangent, gain):
    width = middle.shape[1]
    half = ROWS // 2
    row = pl.BlockSpec((half, width), lambda i: (i, 0))
    first = pl.BlockSpec((None, None, half, width), lambda i: (0, 0, i, 0))
    return pl.pallas_call(
        middle_back_kernel,
        grid=(2,),
        in_specs=[row, first, pl.BlockSpec((None, half, width), lambda i: (0, i, 0)), row, row, whole((1, width))],
        out_specs=[row, row, whole((8, width))],
        out_shape=[
            jax.ShapeDtypeStruct((ROWS, width), f32),
            jax.ShapeDtypeStruct((ROWS, width), bf16),
            jax.ShapeDtypeStruct((8, width), f32),
        ],
        compiler_params=params(),
        cost_estimate=cost(4e6, 5e6),
        name="middle_back",
    )(middle, part, from_core, from_z, cotangent, gain)


def backward_attention_kernel(place, *refs):
    branch = refs[:4]
    wqkv, wo, low, att, totals, qraw, kraw, cos, sin, qgain, kgain = refs[4:15]
    grads, part, branch_out, qpart, kpart = refs[15:20]
    rows, dk, dv, dq = refs[20:]
    step_id = pl.program_id(0)
    i = pl.num_programs(0) - 1 - step_id
    nq, nk = qraw.shape[1], kraw.shape[1]

    @pl.when(step_id == 0)
    def _():
        dk[...] = jnp.zeros_like(dk)
        dv[...] = jnp.zeros_like(dv)
        qpart[...] = jnp.zeros_like(qpart)
        kpart[...] = jnp.zeros_like(kpart)

    pick(place[i], branch, rows)
    b = rows[...]
    branch_out[...] = b
    grad_att = matmul(b, wo[...]).astype(bf16)
    here = pl.ds(pl.multiple_of(i * ROWS, ROWS), ROWS)
    c, s = cos[...], sin[...]
    mask_k = lax.broadcasted_iota(jnp.int32, (ROWS, GROUP * ROWS), 0)
    mask_q = lax.broadcasted_iota(jnp.int32, (ROWS, GROUP * ROWS), 1) % ROWS

    def unturned(w):
        return w * c - pltpu.roll(w, HD // 2, 1) * s

    for h in range(nk // HD):
        cols = [(h * GROUP + a) * HD for a in range(GROUP)]
        q2 = jnp.concatenate([low[here, col : col + HD] for col in cols], axis=0)
        g2 = jnp.concatenate([grad_att[:, col : col + HD] for col in cols], axis=0)
        o2 = jnp.concatenate([att[:, col : col + HD] for col in cols], axis=0)
        total = totals[0, h : h + 1, :]
        dot = jnp.sum((g2.astype(f32) * o2.astype(f32)).T, axis=0, keepdims=True)
        kcol = slice(nq + h * HD, nq + (h + 1) * HD)
        vcol = slice(nq + nk + h * HD, nq + nk + (h + 1) * HD)

        def block(there, masked, h=h, q2=q2, g2=g2, total=total, dot=dot, kcol=kcol, vcol=vcol):
            k = low[there, kcol]
            v = low[there, vcol]
            probs = jnp.exp2(matmul_t(k, q2) * log2_scale - total)
            if masked:
                probs = jnp.where(mask_k <= mask_q, probs, 0.0)
            grad_scores = (probs * (matmul_t(v, g2) - dot)).astype(bf16)
            dv[h, there, :] += matmul(probs.astype(bf16), g2)
            dk[h, there, :] += matmul(grad_scores, q2)
            return t_matmul(grad_scores, k)

        dq[...] = block(here, True)

        def step(j, _, block=block):
            dq[...] += block(pl.ds(pl.multiple_of(j * ROWS, ROWS), ROWS), False)
            return 0

        lax.fori_loop(0, i, step, 0)
        for a, col in enumerate(cols):
            w = unturned(dq[a * ROWS : (a + 1) * ROWS, :] * score_scale)
            grad, gp = norm_back(qraw[:, col : col + HD], qgain[...], w)
            grads[:, col : col + HD] = grad.astype(bf16)
            qpart[:1, :] += gp
        w = unturned(dk[h, here, :] * score_scale)
        grad, gp = norm_back(kraw[:, h * HD : (h + 1) * HD], kgain[...], w)
        grads[:, kcol] = grad.astype(bf16)
        kpart[:1, :] += gp
        grads[:, vcol] = dv[h, here, :].astype(bf16)
    part[0] = matmul_t(grads[...], wqkv[...]).astype(bf16)


def backward_attention(place, branch, weights, low, att, totals, qraw, kraw, cos, sin, qgain, kgain):
    n, width = 4, branch[0].shape[1]
    length, nqkv = low.shape
    nq, nk = qraw.shape[1], kraw.shape[1]
    row = lambda cols: pl.BlockSpec((ROWS, cols), lambda i, p: (n - 1 - i, 0))
    out = [
        ((length, nqkv), bf16, row(nqkv)),
        ((n, ROWS, width), bf16, pl.BlockSpec((1, ROWS, width), lambda i, p: (p[n - 1 - i], 0, 0))),
        ((length, width), bf16, row(width)),
        ((8, HD), f32, whole((8, HD))),
        ((8, HD), f32, whole((8, HD))),
    ]
    return pl.pallas_call(
        backward_attention_kernel,
        grid_spec=pltpu.PrefetchScalarGridSpec(
            num_scalar_prefetch=1,
            grid=(n,),
            in_specs=[
                *[whole((ROWS, width))] * 4,
                whole((width, nqkv)),
                whole((width, nq), (0, nqkv // nq)),
                whole((length, nqkv)),
                row(nq),
                pl.BlockSpec((1, 8, GROUP * ROWS), lambda i, p: (n - 1 - i, 0, 0)),
                row(nq),
                row(nk),
                row(HD),
                row(HD),
                whole((1, HD)),
                whole((1, HD)),
            ],
            out_specs=[o[2] for o in out],
            scratch_shapes=[
                pltpu.VMEM((ROWS, width), bf16),
                pltpu.VMEM((nk // HD, length, HD), f32),
                pltpu.VMEM((nk // HD, length, HD), f32),
                pltpu.VMEM((GROUP * ROWS, HD), f32),
            ],
        ),
        out_shape=[jax.ShapeDtypeStruct(o[0], o[1]) for o in out],
        compiler_params=params(),
        cost_estimate=cost(9e9, 18e6, 3e6),
        name="backward_attention",
    )(place, *branch, weights, weights, low, att, totals, qraw, kraw, cos, sin, qgain, kgain)


def projection_weights_kernel(first, branch, grads, att, out):
    wide = grads.shape[1]
    out[:, :wide] = t_matmul(first[...], grads[...]).astype(bf16)
    out[:, wide:] = t_matmul(branch[...], att[...]).astype(bf16)


def projection_weights(first, branch, grads, att):
    length, width = first.shape
    wide, nq = grads.shape[1], att.shape[1]
    return pl.pallas_call(
        projection_weights_kernel,
        grid=(width // 256,),
        in_specs=[
            pl.BlockSpec((length, 256), lambda i: (0, i)),
            pl.BlockSpec((length, 256), lambda i: (0, i)),
            whole((length, wide)),
            whole((length, nq)),
        ],
        out_specs=pl.BlockSpec((256, wide + nq), lambda i: (i, 0)),
        out_shape=jax.ShapeDtypeStruct((width, wide + nq), bf16),
        compiler_params=params(),
        cost_estimate=cost(3.2e9, 10e6),
        name="projection_weights",
    )(first, branch, grads, att)


def tokens_back_kernel(tokens, mine, from_core, from_z, grad_middle, gain, grad_tokens, gain_part):
    u = mine[...].astype(f32) + from_core[...].astype(f32) + from_z[...].astype(f32)
    grad, part = norm_back(tokens[...].astype(f32), gain[...], u)
    grad_tokens[...] = grad_middle[...] + grad

    @pl.when(pl.program_id(0) == 0)
    def _():
        gain_part[...] = jnp.zeros_like(gain_part)

    gain_part[:1, :] += part


def tokens_back(tokens, part, from_core, from_z, grad_middle, gain):
    width = tokens.shape[1]
    half = ROWS // 2
    row = pl.BlockSpec((half, width), lambda i: (i, 0))
    first = pl.BlockSpec((None, None, half, width), lambda i: (0, 0, i, 0))
    return pl.pallas_call(
        tokens_back_kernel,
        grid=(2,),
        in_specs=[row, first, pl.BlockSpec((None, half, width), lambda i: (0, i, 0)), row, row, whole((1, width))],
        out_specs=[row, whole((8, width))],
        out_shape=[
            jax.ShapeDtypeStruct((ROWS, width), f32),
            jax.ShapeDtypeStruct((8, width), f32),
        ],
        compiler_params=params(),
        cost_estimate=cost(4e6, 4e6),
        name="tokens_back",
    )(tokens, part, from_core, from_z, grad_middle, gain)


def swapped(value, axis):
    return lax.ppermute(value, axis, [(0, 1), (1, 0)])


def tp_gather(own):
    over_z = swapped(own, "zl")
    return [own, over_z, swapped(own, "core"), swapped(over_z, "core")]


def tp_scatter(part):
    part = part.reshape(2, 2, *part.shape[1:])
    from_core = swapped(part[1], "core")
    passed = (part[0, 1].astype(f32) + from_core[1].astype(f32)).astype(bf16)
    return part, from_core, swapped(passed, "zl")


def from_everyone(shard, axes):
    copies = jnp.broadcast_to(shard, (lax.axis_size(axes), *shard.shape))
    return lax.all_to_all(copies, axes, split_axis=0, concat_axis=0, tiled=True)


def summed_rows(part):
    count = lax.axis_size(FSDP)
    blocks = part.reshape(count, part.shape[0] // count, part.shape[1])
    parts = lax.all_to_all(blocks, FSDP, 0, 0, tiled=True)
    return jnp.sum(parts.astype(f32), axis=0)


def rotary_tables(length):
    midway = HD // 2
    frequency = 1.0 / rope_base ** (jnp.arange(midway, dtype=f32) * 2.0 / HD)
    angles = jnp.arange(length, dtype=f32)[:, None] * frequency[None, :]
    cos, sin = jnp.cos(angles), jnp.sin(angles)
    return jnp.concatenate([cos, cos], axis=1), jnp.concatenate([-sin, sin], axis=1)


def local(
    tokens,
    attention_gain,
    query_weight,
    key_weight,
    value_weight,
    query_gain,
    key_gain,
    output_weight,
    feed_gain,
    gate_weight,
    up_weight,
    down_weight,
    cotangent,
):
    count = lax.axis_size(FSDP)
    width = tokens.shape[2]
    nq, nk = query_weight.shape[1], key_weight.shape[1]
    units = gate_weight.shape[1]
    rows = query_weight.shape[0]
    x = tokens[0]
    dy = cotangent[0]
    zl, core = lax.axis_index("zl"), lax.axis_index("core")
    block = jnp.arange(4, dtype=jnp.int32)
    place = ((block % 2) ^ core) * 2 + ((block // 2) ^ zl)
    place = place.astype(jnp.int32)
    cos, sin = rotary_tables(4 * ROWS)

    gains = jnp.concatenate([attention_gain, feed_gain, query_gain, key_gain])
    gains = jnp.pad(gains, (0, -gains.shape[0] % 128))[None]
    gains = from_everyone(gains, FSDP)[:, 0].astype(f32)
    heads = query_gain.shape[0]
    first_gain = gains[:, :rows].reshape(1, width)
    second_gain = gains[:, rows : 2 * rows].reshape(1, width)
    qgain = gains[:, 2 * rows : 2 * rows + heads].reshape(1, HD)
    kgain = gains[:, 2 * rows + heads : 2 * rows + 2 * heads].reshape(1, HD)

    weights = jnp.concatenate([query_weight, key_weight, value_weight, output_weight], axis=1)
    weights = from_everyone(weights, FSDP).reshape(width, -1)
    feed = jnp.concatenate([gate_weight, up_weight, down_weight], axis=1)
    feed = lax.all_gather(feed, FSDP, axis=0, tiled=True)

    token_blocks = tp_gather(x)
    grad_blocks = tp_gather(dy)

    first, qraw, kraw, low, att, totals, part = forward_attention(
        place, token_blocks, first_gain, qgain, kgain, weights, nq, nk, cos, sin
    )
    middle, second = middle_step(x, *tp_scatter(part), second_gain)
    second_blocks = tp_gather(second)
    hidden, grad_units, part = feed_step(second_blocks, grad_blocks, feed, units)
    grad_middle, branch, feed_gain_part = middle_back(middle, *tp_scatter(part), dy, second_gain)
    feed_sums = summed_rows(feed_weights(second_blocks, grad_blocks, grad_units, hidden))

    mine, from_core, from_z = tp_scatter(feed_out(hidden, feed))
    output = middle + mine[0, 0].astype(f32) + from_core[0].astype(f32) + from_z.astype(f32)
    output = output.astype(bf16)

    branch_blocks = tp_gather(branch)
    grads, part, branch_rows, qpart, kpart = backward_attention(
        place, branch_blocks, weights, low, att, totals, qraw, kraw, cos, sin, qgain, kgain
    )
    sums = summed_rows(projection_weights(first, branch_rows, grads, att))
    tokens_grad, first_gain_part = tokens_back(x, *tp_scatter(part), grad_middle, first_gain)

    gain_parts = jnp.concatenate(
        [
            first_gain_part[0].reshape(count, rows),
            feed_gain_part[0].reshape(count, rows),
            qpart[0].reshape(count, heads),
            kpart[0].reshape(count, heads),
        ],
        axis=1,
    )
    gain_parts = jnp.pad(gain_parts, ((0, 0), (0, -gain_parts.shape[1] % 128)))
    gain_parts = jnp.repeat(gain_parts, 4, axis=0)[:, None, :]
    gain_sums = jnp.sum(lax.all_to_all(gain_parts, EVERY, 0, 0, tiled=True), axis=(0, 1))

    return (
        output[None],
        tokens_grad[None],
        gain_sums[:rows],
        sums[:, :nq],
        sums[:, nq : nq + nk],
        sums[:, nq + nk : nq + 2 * nk],
        gain_sums[2 * rows : 2 * rows + heads],
        gain_sums[2 * rows + heads : 2 * rows + 2 * heads],
        sums[:, nq + 2 * nk :],
        gain_sums[rows : 2 * rows],
        feed_sums[:, :units],
        feed_sums[:, units : 2 * units],
        feed_sums[:, 2 * units :],
    )


def solution(mesh):
    fsdp, tp = mesh.devices.shape
    cut = {32: (4, 4, 2), 2: (1, 1, 2), 1: (1, 1, 1)}[fsdp]
    fine = Mesh(mesh.devices.reshape(*cut, 2, tp // 2), EVERY)
    split = ("zl", "core")
    data = P(FSDP, split, None)
    matrix = P(FSDP, split)
    vector = P(FSDP)
    return jax.shard_map(
        local,
        mesh=fine,
        in_specs=(
            data, vector, matrix, matrix, matrix, vector, vector,
            matrix, vector, matrix, matrix, matrix, data,
        ),
        out_specs=(
            data, data, vector, matrix, matrix, matrix, vector, vector,
            matrix, vector, matrix, matrix, matrix,
        ),
        check_vma=False,
    )
```

time: 1140 us -> 441 us (0.39); the launches traced: 1130 us -> 438 us
  waiting for transfers between devices: 577 us -> 215 us
  blocking collectives: 157 us -> 0 us
  local copies, waits for them, and re-layouts: 160 us -> 23.6 us
  matrix products: 105 us -> 0 us
  Pallas kernels: 0 us -> 96.8 us
  other arithmetic: 72 us -> 19.2 us
  starting transfers between devices: 38.6 us -> 69.2 us
    unnamed x7 -> x1, waiting for transfers between devices: 345 us -> 0.02 us
    ppermute x0 -> x20, waiting for transfers between devices: none -> 164 us  [swapped(): return lax.ppermute(value, axis, [(0, 1), (1, 0)])]
    all_to_all x9 -> x5, waiting for transfers between devices: 159 us -> 50.8 us  [the longest x2 45.5 us: summed_rows(): parts = lax.all_to_all(blocks, FSDP, 0, 0, tiled=True)]
    dot_general x33 -> x0, matrix products: 105 us -> none  [the longest x2 9.39 us: attend_backward(): jnp.einsum('hgqk,qhgd->khd', weights_low, grad_block, preferred_element_t...]
    pallas_call x0 -> x9, Pallas kernels: none -> 96.8 us  [the longest x1 26.5 us: backward_attention(): pl.pallas_call(backward_attention_kernel, grid_spec=pltpu.PrefetchScalarG...]
    unnamed x1 -> x0, blocking collectives: 93 us -> none
    all_gather x3 -> x1, waiting for transfers between devices: 72.7 us -> 0.01 us  [local(): feed = lax.all_gather(feed, FSDP, axis=0, tiled=True)]
    all_to_all x3 -> x0, blocking collectives: 63.9 us -> none  [the longest x1 51.7 us: sent_and_summed(): lax.all_to_all(in_blocks(shard, dim, length), axis, 0, 0, tiled=True)]
  transfers between devices with their start and end apart: 14 -> 26, of which waited for: 11 -> 15; matrix products, arithmetic and copies ran while one was open for 16% -> 6% of each run, Pallas kernels for 0% -> 11%
where the time goes in v1:
time: 441 us; the launch traced here: 438 us
  waiting for transfers between devices  215 us (49%)
  Pallas kernels  96.8 us (22%)
  starting transfers between devices  69.2 us (16%)
  local copies, waits for them, and re-layouts  23.6 us (5%)
  other arithmetic  19.2 us (4%)
  between operations  14.3 us (3%)
    ppermute x20, waiting for transfers between devices, swapped(): return lax.ppermute(value, axis, [(0, 1), (1, 0)])  164 us
    all_to_all x2, waiting for transfers between devices, summed_rows(): parts = lax.all_to_all(blocks, FSDP, 0, 0, tiled=True)  45.5 us
    all_to_all x2, starting transfers between devices, summed_rows(): parts = lax.all_to_all(blocks, FSDP, 0, 0, tiled=True)  31 us
    pallas_call x1, Pallas kernels, backward_attention(): pl.pallas_call(backward_attention_kernel, grid_spec=pltpu.PrefetchScalarG...  26.5 us
    pallas_call x1, Pallas kernels, forward_attention(): pl.pallas_call(forward_attention_kernel, grid_spec=pltpu.PrefetchScalarGr...  21.5 us
    all_to_all x2, starting transfers between devices, from_everyone(): return lax.all_to_all(copies, axes, split_axis=0, concat_axis=0, tiled=True)  18.3 us
    pallas_call x1, Pallas kernels, feed_step(): pl.pallas_call(feed_kernel, grid=(4,), in_specs=[*[whole((ROWS, width))]...  16.9 us
    pallas_call x1, Pallas kernels, feed_weights(): pl.pallas_call(feed_weights_kernel, grid=(width // 256,), in_specs=[*[pl....  10 us
  transfers between devices with their start and end apart: 26, of which 15 were waited for; matrix products, arithmetic and copies ran while one was open for 6% of the time, Pallas kernels for 11%

profile of v1, /device:TPU:28, one launch (start us, length us, event | category | flops | bytes accessed | tf_op | source)
XLA Modules:
  0.0 437.7 jit_solution(13168866387356428649)
XLA Ops:
  10.2 10.6 %all-to-all-start = ((bf16[32,1,128]{2,1,0:T(2,128)(2,1)}), bf16[32,1,128]{2,1,0:T(2,128)(2,1)S(1)}, u32[]{:S(2)}, u32[]{:S(2)}) async-start(bf16[32,1,128]{2,1,0:T(2,128)(2,1)} %broadcast_in_dim.18), calls=%async_computation | async-start | bytes 32768 | tf_op jit(solution)/shard_map/all_to_all | solution.py:530
  21.6 5.2 %all-to-all-done = bf16[32,1,128]{2,1,0:T(2,128)(2,1)S(1)} async-done(((bf16[32,1,128]{2,1,0:T(2,128)(2,1)}), bf16[32,1,128]{2,1,0:T(2,128)(2,1)S(1)}, u32[]{:S(2)}, u32[]{:S(2)}) %all-to-all-start) | async-done | bytes 8224 | tf_op jit(solution)/shard_map/all_to_all | solution.py:530
  26.8 2.0 broadcast_in_dim.19
  28.8 7.7 %all-to-all-start.1 = ((bf16[32,32,1536]{2,1,0:T(8,128)(2,1)}), bf16[32,32,1536]{2,1,0:T(8,128)(2,1)S(1)}, u32[]{:S(2)}, u32[]{:S(2)}) async-start(bf16[32,32,1536]{2,1,0:T(8,128)(2,1)} %broadcast_in_dim.19), calls=%async_computation.1 | async-start | bytes 6291456 | tf_op jit(solution)/shard_map/all_to_all | solution.py:530
  40.9 45.0 %collective-permute-done.refs_1_ = bf16[256,1024]{1,0:T(8,128)(2,1)} collective-permute-done((bf16[256,1024]{1,0:T(8,128)(2,1)}, bf16[256,1024]{1,0:T(8,128)(2,1)}, u32[]{:S(2)}, u32[]{:S(2)}) %collective-permute-start) | collective-permute-done | bytes 524320 | tf_op jit(solution)/shard_map/ppermute | solution.py:513
  90.1 21.5 %forward_attention.1 = (bf16[1024,1024]{1,0:T(8,128)(2,1)}, f32[1024,512]{1,0:T(8,128)}, f32[1024,256]{1,0:T(8,128)}, bf16[1024,1024]{1,0:T(8,128)(2,1)}, bf16[1...) custom-call(s32[4]{0:T(128)} %fusion.12.place, bf16[256,1024]{1,0:T(8,128)(2,1)} %bitcast.80, ...), custom_call_target="tpu_custom_call" | custom-call | flops 7000000000 | bytes 16000000 | tf_op jit(solution)/shard_map/forward_attention/pallas_call | solution.py:146
  113.6 2.3 collective-permute-done.3.from_core
  120.3 12.0 %collective-permute-done.4.from_z = bf16[256,1024]{1,0:T(8,128)(2,1)S(1)} collective-permute-done((bf16[256,1024]{1,0:T(8,128)(2,1)S(1)}, bf16[256,1024]{1,0:T(8,128)(2,1)S(1)}, u32[]{:S(2)}, u32[]{:S(2)}) %collective-permute-start.4) | collective-permute-done | bytes 524320 | tf_op jit(solution)/shard_map/ppermute | solution.py:513
  133.1 2.6 middle_step.1
  136.7 6.9 %collective-permute-done.8.refs_5_ = bf16[256,1024]{1,0:T(8,128)(2,1)S(1)} collective-permute-done((bf16[256,1024]{1,0:T(8,128)(2,1)S(1)}, bf16[256,1024]{1,0:T(8,128)(2,1)S(1)}, u32[]{:S(2)}, u32[]{:S(2)}) %collective-permute-start.8) | collective-permute-done | bytes 524320 | tf_op jit(solution)/shard_map/ppermute | solution.py:513
  144.1 10.2 %collective-permute-done.5.refs_1_ = bf16[256,1024]{1,0:T(8,128)(2,1)S(1)} collective-permute-done((bf16[256,1024]{1,0:T(8,128)(2,1)}, bf16[256,1024]{1,0:T(8,128)(2,1)S(1)}, u32[]{:S(2)}, u32[]{:S(2)}) %collective-permute-start.5) | collective-permute-done | bytes 524320 | tf_op jit(solution)/shard_map/ppermute | solution.py:513
  154.3 2.0 collective-permute-done.7.refs_3_
  156.3 16.9 %feed_step.1 = (bf16[1024,768]{1,0:T(8,128)(2,1)}, bf16[1024,1536]{1,0:T(8,128)(2,1)}, bf16[4,256,1024]{2,1,0:T(8,128)(2,1)}) custom-call(bf16[256,1024]{1,0:T(8,128)(2,1)} %get-tuple-element.37.refs_0_, bf16[256,1024]{1,0:T(8,128)(2,1)} %copy-done.10, bf16[256,1024]{1,0:T(8,128)(2,1)} %copy-done.13, bf16[256,1024]{1,0:T(8,128)(2,1)} %collective-permute-done.7.refs_3_, ...), custom_call_target="tpu_custom_call" | custom-call | flops 8000000000 | bytes 16000000 | tf_op jit(solution)/shard_map/feed_step/pallas_call | solution.py:227
  174.7 2.5 collective-permute-done.13.from_core
  179.9 13.0 %collective-permute-done.14.from_z = bf16[256,1024]{1,0:T(8,128)(2,1)S(1)} collective-permute-done((bf16[256,1024]{1,0:T(8,128)(2,1)S(1)}, bf16[256,1024]{1,0:T(8,128)(2,1)S(1)}, u32[]{:S(2)}, u32[]{:S(2)}) %collective-permute-start.14) | collective-permute-done | bytes 524320 | tf_op jit(solution)/shard_map/ppermute | solution.py:513
  193.6 3.1 middle_back.1
  197.8 12.3 %collective-permute-done.15.refs_1_ = bf16[256,1024]{1,0:T(8,128)(2,1)S(1)} collective-permute-done((bf16[256,1024]{1,0:T(8,128)(2,1)}, bf16[256,1024]{1,0:T(8,128)(2,1)S(1)}, u32[]{:S(2)}, u32[]{:S(2)}) %collective-permute-start.15) | collective-permute-done | bytes 524320 | tf_op jit(solution)/shard_map/ppermute | solution.py:513
  212.9 26.5 %backward_attention.1 = (bf16[1024,1024]{1,0:T(8,128)(2,1)}, bf16[4,256,1024]{2,1,0:T(8,128)(2,1)}, bf16[1024,1024]{1,0:T(8,128)(2,1)}, f32[8,128]{1,0:T(8,128)}, f32[8,128]{1,0:T(8,128)}) custom-call(s32[4]{0:T(128)} %fusion.12.place, bf16[256,1024]{1,0:T(8,128)(2,1)} %get-tuple-element.40.refs_0_, bf16[256,1024]{1,0:T(8,128)(2,1)} %copy-done.14, ...), custom_call_target="tpu_custom_call" | custom-call | flops 8999999488 | bytes 18000000 | tf_op jit(solution)/shard_map/backward_attention/pallas_call | solution.py:420
  241.0 2.5 collective-permute-done.18.from_core
  248.6 10.5 %collective-permute-done.19.from_z = bf16[256,1024]{1,0:T(8,128)(2,1)S(1)} collective-permute-done((bf16[256,1024]{1,0:T(8,128)(2,1)S(1)}, bf16[256,1024]{1,0:T(8,128)(2,1)S(1)}, u32[]{:S(2)}, u32[]{:S(2)}) %collective-permute-start.19) | collective-permute-done | bytes 524320 | tf_op jit(solution)/shard_map/ppermute | solution.py:513
  259.9 3.0 tokens_back.1
  264.5 10.0 %all-to-all-start.2 = ((f32[128,1,128]{2,1,0:T(1,128)}), f32[128,1,128]{2,1,0:T(1,128)S(1)}, u32[]{:S(2)}, u32[]{:S(2)}) async-start(f32[128,1,128]{2,1,0:T(1,128)} %bitcast.20), calls=%async_computation.2 | async-start | bytes 131072 | tf_op jit(solution)/shard_map/all_to_all | solution.py:624
  274.5 10.0 %feed_weights.1 = bf16[1024,2304]{1,0:T(8,128)(2,1)} custom-call(bf16[256,1024]{1,0:T(8,128)(2,1)} %get-tuple-element.37.refs_0_, bf16[256,1024]{1,0:T(8,128)(2,1)} %copy-done.10, bf16[256,1024]{1,0:T(8,128)(2,1)} %copy-done.13, bf16[256,1024]{1,0:T(8,128)(2,1)} %collective-permute-done.7.refs_3_, bf16[256,1024]{1,0:T(8,128)(2,1)} %bitcast.85, ...), custom_call_target="tpu_custom_call" | custom-call | flops 4800000000 | bytes 14000000 | tf_op jit(solution)/shard_map/feed_weights/pallas_call | solution.py:288
  284.5 10.3 %all-to-all-start.4 = ((bf16[32,32,2304]{2,1,0:T(8,128)(2,1)}), bf16[32,32,2304]{2,1,0:T(8,128)(2,1)}, u32[]{:S(2)}, u32[]{:S(2)}) async-start(bf16[32,32,2304]{2,1,0:T(8,128)(2,1)} %bitcast.72), calls=%async_computation.4 | async-start | bytes 9437184 | tf_op jit(solution)/shard_map/all_to_all | solution.py:536
  294.9 5.4 %feed_out.1 = bf16[4,256,1024]{2,1,0:T(8,128)(2,1)} custom-call(bf16[1024,768]{1,0:T(8,128)(2,1)} %get-tuple-element.38.hidden.refs_9_, bf16[1024,2304]{1,0:T(8,128)(2,1)} %all-gather.2.cloned.1.call-done.refs_8_.refs_9_.refs_10_.wd), custom_call_target="tpu_custom_call" | custom-call | flops 1600000000 | bytes 5000000 | tf_op jit(solution)/shard_map/feed_out/pallas_call | solution.py:256
  300.3 2.3 slice.143
  302.5 7.8 %projection_weights.1 = bf16[1024,1536]{1,0:T(8,128)(2,1)} custom-call(bf16[1024,1024]{1,0:T(8,128)(2,1)} %get-tuple-element.53.first, bf16[1024,1024]{1,0:T(8,128)(2,1)} %get-tuple-element.54.branch, bf16[1024,1024]{1,0:T(8,128)(2,1)} %get-tuple-element.55.grads, bf16[1024,512]{1,0:T(8,128)(2,1)} %get-tuple-element.42.refs_7_.att), custom_call_target="tpu_custom_call" | custom-call | flops 3200000000 | bytes 10000000 | tf_op jit(solution)/shard_map/projection_weights/pallas_call | solution.py:463
  310.4 45.5 %all-to-all-done.4 = bf16[32,32,2304]{2,1,0:T(8,128)(2,1)} async-done(((bf16[32,32,2304]{2,1,0:T(8,128)(2,1)}), bf16[32,32,2304]{2,1,0:T(8,128)(2,1)}, u32[]{:S(2)}, u32[]{:S(2)}) %all-to-all-start.4) | async-done | bytes 4718624 | tf_op jit(solution)/shard_map/all_to_all | solution.py:536
  355.9 20.7 %all-to-all-start.3 = ((bf16[32,32,1536]{2,1,0:T(8,128)(2,1)}), bf16[32,32,1536]{2,1,0:T(8,128)(2,1)S(1)}, u32[]{:S(2)}, u32[]{:S(2)}) async-start(bf16[32,32,1536]{2,1,0:T(8,128)(2,1)} %bitcast.77), calls=%async_computation.3 | async-start | bytes 6291456 | tf_op jit(solution)/shard_map/all_to_all | solution.py:536
  379.0 42.7 %collective-permute-done.12 = bf16[256,1024]{1,0:T(8,128)(2,1)S(1)} collective-permute-done((bf16[256,1024]{1,0:T(8,128)(2,1)S(1)}, bf16[256,1024]{1,0:T(8,128)(2,1)S(1)}, u32[]{:S(2)}, u32[]{:S(2)}) %collective-permute-start.12) | collective-permute-done | bytes 524320 | tf_op jit(solution)/shard_map/ppermute | solution.py:513
  421.7 2.3 fusion.6
  425.4 3.0 convert_reduce_fusion
  (107 shorter events, 45.0 us)
Async XLA Ops:
  7.2 149.1 %all-gather.2.cloned.1.call-start = ((), (), s32[]{:S(2)}) async-start(), calls=%async_computation.5 | async-start | bytes 4866048 | tf_op jit(solution)/shard_map/all_gather | solution.py:588
  10.2 16.7 %all-to-all-start = ((bf16[32,1,128]{2,1,0:T(2,128)(2,1)}), bf16[32,1,128]{2,1,0:T(2,128)(2,1)S(1)}, u32[]{:S(2)}, u32[]{:S(2)}) async-start(bf16[32,1,128]{2,1,0:T(2,128)(2,1)} %broadcast_in_dim.18), calls=%async_computation | async-start | bytes 32768 | tf_op jit(solution)/shard_map/all_to_all | solution.py:530
  28.8 59.6 %all-to-all-start.1 = ((bf16[32,32,1536]{2,1,0:T(8,128)(2,1)}), bf16[32,32,1536]{2,1,0:T(8,128)(2,1)S(1)}, u32[]{:S(2)}, u32[]{:S(2)}) async-start(bf16[32,32,1536]{2,1,0:T(8,128)(2,1)} %broadcast_in_dim.19), calls=%async_computation.1 | async-start | bytes 6291456 | tf_op jit(solution)/shard_map/all_to_all | solution.py:530
  36.5 49.4 %collective-permute-start = (bf16[256,1024]{1,0:T(8,128)(2,1)}, bf16[256,1024]{1,0:T(8,128)(2,1)}, u32[]{:S(2)}, u32[]{:S(2)}) collective-permute-start(bf16[256,1024]{1,0:T(8,128)(2,1)} %bitcast.78), channel_id=1, source_target_pairs={{0,2},{2,0},{1,3},{3,1},{4,6},{6,4},{5,7},{7,5},{8,10},{10,8},{9,1... | collective-permute-start | bytes 1572872 | tf_op jit(solution)/shard_map/ppermute | solution.py:513
  37.6 50.9 %collective-permute-start.1 = (bf16[256,1024]{1,0:T(8,128)(2,1)}, bf16[256,1024]{1,0:T(8,128)(2,1)}, u32[]{:S(2)}, u32[]{:S(2)}) collective-permute-start(bf16[256,1024]{1,0:T(8,128)(2,1)} %bitcast.79), channel_id=1, source_target_pairs={{0,1},{1,0},{2,3},{3,2},{4,5},{5,4},{6,7},{7,6},{8,9},{9,8},{10,11... | collective-permute-start | bytes 1572872 | tf_op jit(solution)/shard_map/ppermute | solution.py:513
  85.9 2.6 collective-permute-start.2
  111.6 6.9 %copy-start.5 = (bf16[1,256,1024]{2,1,0:T(8,128)(2,1)S(1)}, bf16[1,256,1024]{2,1,0:T(8,128)(2,1)}, u32[]{:S(2)}) copy-start(bf16[1,256,1024]{2,1,0:T(8,128)(2,1)} %param.25) | copy-start | bytes 1572868
  113.0 2.9 collective-permute-start.3
  115.9 16.4 %copy-start.2 = (bf16[2,256,1024]{2,1,0:T(8,128)(2,1)}, bf16[2,256,1024]{2,1,0:T(8,128)(2,1)S(1)}, u32[]{:S(2)}) copy-start(bf16[2,256,1024]{2,1,0:T(8,128)(2,1)S(1)} %collective-permute-done.3.from_core) | copy-start | bytes 3145732
  117.5 14.8 %collective-permute-start.4 = (bf16[256,1024]{1,0:T(8,128)(2,1)S(1)}, bf16[256,1024]{1,0:T(8,128)(2,1)S(1)}, u32[]{:S(2)}, u32[]{:S(2)}) collective-permute-start(bf16[256,1024]{1,0:T(8,128)(2,1)S(1)} %fusion.5), channel_id=1, source_target_pairs={{0,2},{2,0},{1,3},{3,1},{4,6},{6,4},{5,7},{7,5},{8,10},{10,8},{9,1... | collective-permute-start | bytes 1572872 | tf_op jit(solution)/shard_map/ppermute | solution.py:513
  118.6 25.0 %collective-permute-start.8 = (bf16[256,1024]{1,0:T(8,128)(2,1)S(1)}, bf16[256,1024]{1,0:T(8,128)(2,1)S(1)}, u32[]{:S(2)}, u32[]{:S(2)}) collective-permute-start(bf16[256,1024]{1,0:T(8,128)(2,1)S(1)} %bitcast.86), channel_id=1, source_target_pairs={{0,2},{2,0},{1,3},{3,1},{4,6},{6,4},{5,7},{7,5},{8,10},{10,8},{9,1... | collective-permute-start | bytes 1572872 | tf_op jit(solution)/shard_map/ppermute | solution.py:513
  135.7 18.6 %collective-permute-start.5 = (bf16[256,1024]{1,0:T(8,128)(2,1)}, bf16[256,1024]{1,0:T(8,128)(2,1)S(1)}, u32[]{:S(2)}, u32[]{:S(2)}) collective-permute-start(bf16[256,1024]{1,0:T(8,128)(2,1)} %get-tuple-element.37.refs_0_), channel_id=1, source_target_pairs={{0,2},{2,0},{1,3},{3,1},{4,6},{6,4},{5,7},{7,5},{8,10},{10,8},{9,1... | collective-permute-start | bytes 1572872 | tf_op jit(solution)/shard_map/ppermute | solution.py:513
  136.7 17.6 %collective-permute-start.9 = (bf16[256,1024]{1,0:T(8,128)(2,1)S(1)}, bf16[256,1024]{1,0:T(8,128)(2,1)S(1)}, u32[]{:S(2)}, u32[]{:S(2)}) collective-permute-start(bf16[256,1024]{1,0:T(8,128)(2,1)S(1)} %bitcast.87), channel_id=1, source_target_pairs={{0,1},{1,0},{2,3},{3,2},{4,5},{5,4},{6,7},{7,6},{8,9},{9,8},{10,11... | collective-permute-start | bytes 1572872 | tf_op jit(solution)/shard_map/ppermute | solution.py:513
  143.6 12.7 %copy-start.9 = (bf16[256,1024]{1,0:T(8,128)(2,1)}, bf16[256,1024]{1,0:T(8,128)(2,1)S(1)}, u32[]{:S(2)}) copy-start(bf16[256,1024]{1,0:T(8,128)(2,1)S(1)} %collective-permute-done.8.refs_5_) | copy-start | bytes 1572868
  143.6 10.7 %collective-permute-start.10 = (bf16[256,1024]{1,0:T(8,128)(2,1)S(1)}, bf16[256,1024]{1,0:T(8,128)(2,1)S(1)}, u32[]{:S(2)}, u32[]{:S(2)}) collective-permute-start(bf16[256,1024]{1,0:T(8,128)(2,1)S(1)} %collective-permute-done.8.refs_5_), channel_id=1, source_target_pairs={{0,1},{1,0},{2,3},{3,2},{4,5},{5,4},{6,7},{7,6},{8,9},{9,8},{10,11... | collective-permute-start | bytes 1572872 | tf_op jit(solution)/shard_map/ppermute | solution.py:513
  143.6 10.7 %collective-permute-start.6 = (bf16[256,1024]{1,0:T(8,128)(2,1)}, bf16[256,1024]{1,0:T(8,128)(2,1)S(1)}, u32[]{:S(2)}, u32[]{:S(2)}) collective-permute-start(bf16[256,1024]{1,0:T(8,128)(2,1)} %get-tuple-element.37.refs_0_), channel_id=1, source_target_pairs={{0,1},{1,0},{2,3},{3,2},{4,5},{5,4},{6,7},{7,6},{8,9},{9,8},{10,11... | collective-permute-start | bytes 1572872 | tf_op jit(solution)/shard_map/ppermute | solution.py:513
  154.2 2.0 collective-permute-start.7
  174.5 2.7 collective-permute-start.13
  177.2 15.6 %copy-start.4 = (bf16[2,256,1024]{2,1,0:T(8,128)(2,1)}, bf16[2,256,1024]{2,1,0:T(8,128)(2,1)S(1)}, u32[]{:S(2)}) copy-start(bf16[2,256,1024]{2,1,0:T(8,128)(2,1)S(1)} %collective-permute-done.13.from_core) | copy-start | bytes 3145732
  178.8 14.0 %collective-permute-start.14 = (bf16[256,1024]{1,0:T(8,128)(2,1)S(1)}, bf16[256,1024]{1,0:T(8,128)(2,1)S(1)}, u32[]{:S(2)}, u32[]{:S(2)}) collective-permute-start(bf16[256,1024]{1,0:T(8,128)(2,1)S(1)} %fusion.1), channel_id=1, source_target_pairs={{0,2},{2,0},{1,3},{3,1},{4,6},{6,4},{5,7},{7,5},{8,10},{10,8},{9,1... | collective-permute-start | bytes 1572872 | tf_op jit(solution)/shard_map/ppermute | solution.py:513
  196.8 13.4 %collective-permute-start.15 = (bf16[256,1024]{1,0:T(8,128)(2,1)}, bf16[256,1024]{1,0:T(8,128)(2,1)S(1)}, u32[]{:S(2)}, u32[]{:S(2)}) collective-permute-start(bf16[256,1024]{1,0:T(8,128)(2,1)} %get-tuple-element.40.refs_0_), channel_id=1, source_target_pairs={{0,2},{2,0},{1,3},{3,1},{4,6},{6,4},{5,7},{7,5},{8,10},{10,8},{9,1... | collective-permute-start | bytes 1572872 | tf_op jit(solution)/shard_map/ppermute | solution.py:513
  197.8 12.4 %collective-permute-start.16 = (bf16[256,1024]{1,0:T(8,128)(2,1)}, bf16[256,1024]{1,0:T(8,128)(2,1)S(1)}, u32[]{:S(2)}, u32[]{:S(2)}) collective-permute-start(bf16[256,1024]{1,0:T(8,128)(2,1)} %get-tuple-element.40.refs_0_), channel_id=1, source_target_pairs={{0,1},{1,0},{2,3},{3,2},{4,5},{5,4},{6,7},{7,6},{8,9},{9,8},{10,11... | collective-permute-start | bytes 1572872 | tf_op jit(solution)/shard_map/ppermute | solution.py:513
  210.2 1.9 collective-permute-start.17
  240.8 2.7 collective-permute-start.18
  243.5 15.6 %copy-start.3 = (bf16[2,256,1024]{2,1,0:T(8,128)(2,1)}, bf16[2,256,1024]{2,1,0:T(8,128)(2,1)S(1)}, u32[]{:S(2)}) copy-start(bf16[2,256,1024]{2,1,0:T(8,128)(2,1)S(1)} %collective-permute-done.18.from_core) | copy-start | bytes 3145732
  245.1 14.0 %collective-permute-start.19 = (bf16[256,1024]{1,0:T(8,128)(2,1)S(1)}, bf16[256,1024]{1,0:T(8,128)(2,1)S(1)}, u32[]{:S(2)}, u32[]{:S(2)}) collective-permute-start(bf16[256,1024]{1,0:T(8,128)(2,1)S(1)} %fusion), channel_id=1, source_target_pairs={{0,2},{2,0},{1,3},{3,1},{4,6},{6,4},{5,7},{7,5},{8,10},{10,8},{9,1... | collective-permute-start | bytes 1572872 | tf_op jit(solution)/shard_map/ppermute | solution.py:513
  264.5 20.0 %all-to-all-start.2 = ((f32[128,1,128]{2,1,0:T(1,128)}), f32[128,1,128]{2,1,0:T(1,128)S(1)}, u32[]{:S(2)}, u32[]{:S(2)}) async-start(f32[128,1,128]{2,1,0:T(1,128)} %bitcast.20), calls=%async_computation.2 | async-start | bytes 131072 | tf_op jit(solution)/shard_map/all_to_all | solution.py:624
  284.5 71.4 %all-to-all-start.4 = ((bf16[32,32,2304]{2,1,0:T(8,128)(2,1)}), bf16[32,32,2304]{2,1,0:T(8,128)(2,1)}, u32[]{:S(2)}, u32[]{:S(2)}) async-start(bf16[32,32,2304]{2,1,0:T(8,128)(2,1)} %bitcast.72), calls=%async_computation.4 | async-start | bytes 9437184 | tf_op jit(solution)/shard_map/all_to_all | solution.py:536
  302.5 74.1 %collective-permute-start.11 = (bf16[2,256,1024]{2,1,0:T(8,128)(2,1)}, bf16[2,256,1024]{2,1,0:T(8,128)(2,1)}, u32[]{:S(2)}, u32[]{:S(2)}) collective-permute-start(bf16[2,256,1024]{2,1,0:T(8,128)(2,1)} %slice.143), channel_id=1, source_target_pairs={{0,1},{1,0},{2,3},{3,2},{4,5},{5,4},{6,7},{7,6},{8,9},{9,8},{10,11... | collective-permute-start | bytes 3145736 | tf_op jit(solution)/shard_map/ppermute | solution.py:513
  355.9 73.3 %all-to-all-start.3 = ((bf16[32,32,1536]{2,1,0:T(8,128)(2,1)}), bf16[32,32,1536]{2,1,0:T(8,128)(2,1)S(1)}, u32[]{:S(2)}, u32[]{:S(2)}) async-start(bf16[32,32,1536]{2,1,0:T(8,128)(2,1)} %bitcast.77), calls=%async_computation.3 | async-start | bytes 6291456 | tf_op jit(solution)/shard_map/all_to_all | solution.py:536
  376.6 45.2 %copy-start = (f32[256,1024]{1,0:T(8,128)S(1)}, f32[256,1024]{1,0:T(8,128)}, u32[]{:S(2)}) copy-start(f32[256,1024]{1,0:T(8,128)} %get-tuple-element.36.middle) | copy-start | bytes 3145732
  378.1 43.7 %collective-permute-start.12 = (bf16[256,1024]{1,0:T(8,128)(2,1)S(1)}, bf16[256,1024]{1,0:T(8,128)(2,1)S(1)}, u32[]{:S(2)}, u32[]{:S(2)}) collective-permute-start(bf16[256,1024]{1,0:T(8,128)(2,1)S(1)} %fusion.2), channel_id=1, source_target_pairs={{0,2},{2,0},{1,3},{3,1},{4,6},{6,4},{5,7},{7,5},{8,10},{10,8},{9,1... | collective-permute-start | bytes 1572872 | tf_op jit(solution)/shard_map/ppermute | solution.py:513
  (11 other events, 16.8 us)
Sparse Core Ops, SparseCore 0:
  11.0 112.7 all-gather.1

commit v2 on v1

--- a/solution.py
+++ b/solution.py
@@ -1,3 +1,4 @@
+import functools
 import math
 
 import jax
@@ -9,6 +10,7 @@
 
 HD = 128
 ROWS = 256
+WIDTH = 1024
 GROUP = 2
 epsilon = 1e-06
 rope_base = 1000000.0
@@ -49,7 +51,7 @@
 
 
 def cost(flops, nbytes, trans=0):
-    return pl.CostEstimate(flops=int(flops), bytes_accessed=int(nbytes), transcendentals=int(trans))
+    return pl.CostEstimate(flops=int(flops / 8), bytes_accessed=int(nbytes / 8), transcendentals=int(trans / 8))
 
 
 def whole(shape, index=None):
@@ -57,6 +59,13 @@
     return pl.BlockSpec(shape, lambda i, *_: index)
 
 
+def halves(width):
+    return [
+        pl.BlockSpec((1, ROWS, width), lambda i: (jnp.minimum(i, 1), 0, 0)),
+        pl.BlockSpec((1, ROWS, width), lambda i: (jnp.maximum(i - 2, 0), 0, 0)),
+    ]
+
+
 def pick(which, pieces, target):
     for k, piece in enumerate(pieces):
 
@@ -65,15 +74,62 @@
             target[...] = piece[...]
 
 
-def forward_attention_kernel(place, *refs):
+def equal_iota(rows, cols, make):
+    r = lax.broadcasted_iota(jnp.int32, (rows, cols), 0)
+    c = lax.broadcasted_iota(jnp.int32, (rows, cols), 1)
+    return make(r, c)
+
+
+def row_of(columns, k):
+    same = equal_iota(128, 128, lambda r, c: r == c)
+    parts = []
+    for m in range(columns.shape[0] // 128):
+        col = columns[m * 128 : (m + 1) * 128, k : k + 1].astype(f32)
+        parts.append(jnp.sum(jnp.where(same, col, 0.0), axis=0, keepdims=True))
+    return jnp.concatenate(parts, axis=1)
+
+
+def of_head(rows, per_device, first_row=0):
+    held = HD * per_device // WIDTH
+    return equal_iota(
+        rows, HD, lambda r, c: ((r + first_row) // per_device * held + (r + first_row) % per_device == c)
+        & ((r + first_row) % per_device < held)
+    )
+
+
+def heads_of(columns, k, per_device):
+    col = columns[:, k : k + 1].astype(f32)
+    return jnp.sum(jnp.where(of_head(columns.shape[0], per_device), col, 0.0), axis=0, keepdims=True)
+
+
+def put(which, value, mine, other):
+    @pl.when(which < 2)
+    def _():
+        mine[0] = value
+
+    @pl.when(which >= 2)
+    def _():
+        other[0] = value
+
+
+def forward_attention_kernel(per_device, place, *refs):
     tokens = refs[:4]
-    gain, qgain, kgain, wqkv, wo, cos, sin = refs[4:11]
-    first, qraw, kraw, low, att, totals, part = refs[11:18]
-    rows, keys, values, acc = refs[18:]
+    columns, wqkv, wo, cos, sin = refs[4:9]
+    first, qraw, kraw, low, att, totals, mine, other, gains, head_gains = refs[9:19]
+    rows, keys, values, acc = refs[19:]
     i = pl.program_id(0)
+
+    @pl.when(i == 0)
+    def _():
+        gains[:2, :] = jnp.concatenate([row_of(columns, 0), row_of(columns, 1)], axis=0)
+        gains[2:, :] = jnp.zeros_like(gains[2:, :])
+        head_gains[:2, :] = jnp.concatenate([heads_of(columns, k, per_device) for k in (2, 3)], axis=0)
+        head_gains[2:, :] = jnp.zeros_like(head_gains[2:, :])
+
+    gain, qgain, kgain = gains[:1, :], head_gains[:1, :], head_gains[1:2, :]
     pick(place[i], tokens, rows)
     x = rows[...].astype(f32)
-    normed = (x * inverse_rms(x) * gain[...]).astype(bf16)
+    normed = (x * inverse_rms(x) * gain).astype(bf16)
     first[...] = normed
     qkv = matmul(normed, wqkv[...])
     nq = qraw.shape[1]
@@ -88,7 +144,7 @@
         return (n * c + pltpu.roll(n, HD // 2, 1) * s).astype(bf16)
 
     for h in range(nk // HD):
-        k_low = turned(qkv[:, nq + h * HD : nq + (h + 1) * HD], kgain[...])
+        k_low = turned(qkv[:, nq + h * HD : nq + (h + 1) * HD], kgain)
         v_low = qkv[:, nq + nk + h * HD : nq + nk + (h + 1) * HD].astype(bf16)
         low[:, nq + h * HD : nq + (h + 1) * HD] = k_low
         low[:, nq + nk + h * HD : nq + nk + (h + 1) * HD] = v_low
@@ -103,7 +159,7 @@
         qs = []
         for a in range(GROUP):
             col = (h * GROUP + a) * HD
-            q_low = turned(qkv[:, col : col + HD], qgain[...])
+            q_low = turned(qkv[:, col : col + HD], qgain)
             low[:, col : col + HD] = q_low
             qs.append(q_low)
         q2 = jnp.concatenate(qs, axis=0)
@@ -126,10 +182,10 @@
     totals[0] = jnp.concatenate(sums + [jnp.zeros((8 - len(sums), GROUP * ROWS), f32)], axis=0)
     together = jnp.concatenate(outs, axis=1)
     att[...] = together
-    part[0] = matmul_t(together, wo[...]).astype(bf16)
-
-
-def forward_attention(place, tokens, gain, qgain, kgain, weights, nq, nk, cos, sin):
+    put(place[i], matmul_t(together, wo[...]).astype(bf16), mine, other)
+
+
+def forward_attention(place, tokens, weights, nq, nk, cos, sin):
     n, width = 4, tokens[0].shape[1]
     length = n * ROWS
     nqkv = nq + 2 * nk
@@ -141,18 +197,18 @@
         ((length, nqkv), bf16, row(nqkv)),
         ((length, nq), bf16, row(nq)),
         ((n, 8, GROUP * ROWS), f32, pl.BlockSpec((1, 8, GROUP * ROWS), lambda i, p: (i, 0, 0))),
-        ((n, ROWS, width), bf16, pl.BlockSpec((1, ROWS, width), lambda i, p: (p[i], 0, 0))),
+        *[((2, ROWS, width), bf16, pl.BlockSpec((1, ROWS, width), lambda i, p: (p[i] % 2, 0, 0)))] * 2,
+        ((8, width), f32, whole((8, width))),
+        ((8, HD), f32, whole((8, HD))),
     ]
     return pl.pallas_call(
-        forward_attention_kernel,
+        functools.partial(forward_attention_kernel, width // lax.axis_size(FSDP)),
         grid_spec=pltpu.PrefetchScalarGridSpec(
             num_scalar_prefetch=1,
             grid=(n,),
             in_specs=[
                 *[whole((ROWS, width))] * 4,
-                whole((1, width)),
-                whole((1, HD)),
-                whole((1, HD)),
+                whole((width, HD), (0, (nqkv + nq) // HD)),
                 whole((width, nqkv)),
                 whole((width, nq), (0, nqkv // nq)),
                 row(HD),
@@ -170,25 +226,25 @@
         compiler_params=params(),
         cost_estimate=cost(7e9, 16e6, 3e6),
         name="forward_attention",
-    )(place, *tokens, gain, qgain, kgain, weights, weights, cos, sin)
+    )(place, *tokens, weights, weights, weights, cos, sin)
 
 
 def middle_kernel(tokens, mine, from_core, from_z, gain, middle, second):
     total = mine[...].astype(f32) + from_core[...].astype(f32) + from_z[...].astype(f32)
     v = tokens[...].astype(f32) + total
     middle[...] = v
-    second[...] = (v * inverse_rms(v) * gain[...]).astype(bf16)
+    second[...] = (v * inverse_rms(v) * gain[1:2, :]).astype(bf16)
 
 
 def middle_step(tokens, part, from_core, from_z, gain):
     width = tokens.shape[1]
     half = ROWS // 2
     row = pl.BlockSpec((half, width), lambda i: (i, 0))
-    first = pl.BlockSpec((None, None, half, width), lambda i: (0, 0, i, 0))
+    first = pl.BlockSpec((None, half, width), lambda i: (0, i, 0))
     return pl.pallas_call(
         middle_kernel,
         grid=(2,),
-        in_specs=[row, first, pl.BlockSpec((None, half, width), lambda i: (0, i, 0)), row, whole((1, width))],
+        in_specs=[row, first, first, row, whole((8, width))],
         out_specs=[row, row],
         out_shape=[jax.ShapeDtypeStruct((ROWS, width), f32), jax.ShapeDtypeStruct((ROWS, width), bf16)],
         compiler_params=params(),
@@ -200,8 +256,8 @@
 def feed_kernel(*refs):
     second, grads = refs[:4], refs[4:8]
     wg, wu, wd = refs[8:11]
-    hidden, grad_units, part = refs[11:14]
-    rows_s, rows_g = refs[14:]
+    hidden, grad_units, mine, other = refs[11:15]
+    rows_s, rows_g = refs[15:]
     i = pl.program_id(0)
     pick(i, second, rows_s)
     pick(i, grads, rows_g)
@@ -217,7 +273,7 @@
     units = wg.shape[1]
     grad_units[:, :units] = gg
     grad_units[:, units:] = gu
-    part[0] = (matmul_t(gg, wg[...]) + matmul_t(gu, wu[...])).astype(bf16)
+    put(i, (matmul_t(gg, wg[...]) + matmul_t(gu, wu[...])).astype(bf16), mine, other)
 
 
 def feed_step(second, grads, weights, units):
@@ -233,11 +289,11 @@
             whole((width, units), (0, 1)),
             whole((width, units), (0, 2)),
         ],
-        out_specs=[row(units), row(2 * units), pl.BlockSpec((1, ROWS, width), lambda i: (i, 0, 0))],
+        out_specs=[row(units), row(2 * units), *halves(width)],
         out_shape=[
             jax.ShapeDtypeStruct((length, units), bf16),
             jax.ShapeDtypeStruct((length, 2 * units), bf16),
-            jax.ShapeDtypeStruct((4, ROWS, width), bf16),
+            *[jax.ShapeDtypeStruct((2, ROWS, width), bf16)] * 2,
         ],
         scratch_shapes=[pltpu.VMEM((ROWS, width), bf16)] * 2,
         compiler_params=params(),
@@ -246,8 +302,8 @@
     )(*second, *grads, weights, weights, weights)
 
 
-def feed_out_kernel(hidden, wd, part):
-    part[0] = matmul_t(hidden[...], wd[...]).astype(bf16)
+def feed_out_kernel(hidden, wd, mine, other):
+    put(pl.program_id(0), matmul_t(hidden[...], wd[...]).astype(bf16), mine, other)
 
 
 def feed_out(hidden, weights):
@@ -257,8 +313,8 @@
         feed_out_kernel,
         grid=(4,),
         in_specs=[pl.BlockSpec((ROWS, units), lambda i: (i, 0)), whole((width, units), (0, 2))],
-        out_specs=pl.BlockSpec((1, ROWS, width), lambda i: (i, 0, 0)),
-        out_shape=jax.ShapeDtypeStruct((4, ROWS, width), bf16),
+        out_specs=halves(width),
+        out_shape=[jax.ShapeDtypeStruct((2, ROWS, width), bf16)] * 2,
         compiler_params=params(),
         cost_estimate=cost(1.6e9, 5e6),
         name="feed_out",
@@ -303,7 +359,7 @@
 
 def middle_back_kernel(middle, mine, from_core, from_z, cotangent, gain, grad_middle, branch, gain_part):
     u = mine[...].astype(f32) + from_core[...].astype(f32) + from_z[...].astype(f32)
-    grad, part = norm_back(middle[...], gain[...], u)
+    grad, part = norm_back(middle[...], gain[1:2, :], u)
     grad = cotangent[...].astype(f32) + grad
     grad_middle[...] = grad
     branch[...] = grad.astype(bf16)
@@ -319,11 +375,11 @@
     width = middle.shape[1]
     half = ROWS // 2
     row = pl.BlockSpec((half, width), lambda i: (i, 0))
-    first = pl.BlockSpec((None, None, half, width), lambda i: (0, 0, i, 0))
+    first = pl.BlockSpec((None, half, width), lambda i: (0, i, 0))
     return pl.pallas_call(
         middle_back_kernel,
         grid=(2,),
-        in_specs=[row, first, pl.BlockSpec((None, half, width), lambda i: (0, i, 0)), row, row, whole((1, width))],
+        in_specs=[row, first, first, row, row, whole((8, width))],
         out_specs=[row, row, whole((8, width))],
         out_shape=[
             jax.ShapeDtypeStruct((ROWS, width), f32),
@@ -338,9 +394,11 @@
 
 def backward_attention_kernel(place, *refs):
     branch = refs[:4]
-    wqkv, wo, low, att, totals, qraw, kraw, cos, sin, qgain, kgain = refs[4:15]
-    grads, part, branch_out, qpart, kpart = refs[15:20]
-    rows, dk, dv, dq = refs[20:]
+    tokens = refs[4:8]
+    wqkv, wo, low, att, totals, qraw, kraw, cos, sin, head_gains = refs[8:18]
+    grads, mine, other, branch_out, gain_part, head_part = refs[18:24]
+    rows, xs, dk, dv, dq = refs[24:]
+    qgain, kgain = head_gains[:1, :], head_gains[1:2, :]
     step_id = pl.program_id(0)
     i = pl.num_programs(0) - 1 - step_id
     nq, nk = qraw.shape[1], kraw.shape[1]
@@ -349,10 +407,11 @@
     def _():
         dk[...] = jnp.zeros_like(dk)
         dv[...] = jnp.zeros_like(dv)
-        qpart[...] = jnp.zeros_like(qpart)
-        kpart[...] = jnp.zeros_like(kpart)
+        gain_part[...] = jnp.zeros_like(gain_part)
+        head_part[...] = jnp.zeros_like(head_part)
 
     pick(place[i], branch, rows)
+    pick(place[i], tokens, xs)
     b = rows[...]
     branch_out[...] = b
     grad_att = matmul(b, wo[...]).astype(bf16)
@@ -394,27 +453,30 @@
         lax.fori_loop(0, i, step, 0)
         for a, col in enumerate(cols):
             w = unturned(dq[a * ROWS : (a + 1) * ROWS, :] * score_scale)
-            grad, gp = norm_back(qraw[:, col : col + HD], qgain[...], w)
+            grad, gp = norm_back(qraw[:, col : col + HD], qgain, w)
             grads[:, col : col + HD] = grad.astype(bf16)
-            qpart[:1, :] += gp
+            head_part[:1, :] += gp
         w = unturned(dk[h, here, :] * score_scale)
-        grad, gp = norm_back(kraw[:, h * HD : (h + 1) * HD], kgain[...], w)
+        grad, gp = norm_back(kraw[:, h * HD : (h + 1) * HD], kgain, w)
         grads[:, kcol] = grad.astype(bf16)
-        kpart[:1, :] += gp
+        head_part[1:2, :] += gp
         grads[:, vcol] = dv[h, here, :].astype(bf16)
-    part[0] = matmul_t(grads[...], wqkv[...]).astype(bf16)
-
-
-def backward_attention(place, branch, weights, low, att, totals, qraw, kraw, cos, sin, qgain, kgain):
+    upstream = matmul_t(grads[...], wqkv[...])
+    put(place[i], upstream.astype(bf16), mine, other)
+    x = xs[...].astype(f32)
+    gain_part[:1, :] += jnp.sum(upstream * x * inverse_rms(x), axis=0, keepdims=True)
+
+
+def backward_attention(place, branch, tokens, weights, low, att, totals, qraw, kraw, cos, sin, head_gains):
     n, width = 4, branch[0].shape[1]
     length, nqkv = low.shape
     nq, nk = qraw.shape[1], kraw.shape[1]
     row = lambda cols: pl.BlockSpec((ROWS, cols), lambda i, p: (n - 1 - i, 0))
     out = [
         ((length, nqkv), bf16, row(nqkv)),
-        ((n, ROWS, width), bf16, pl.BlockSpec((1, ROWS, width), lambda i, p: (p[n - 1 - i], 0, 0))),
+        *[((2, ROWS, width), bf16, pl.BlockSpec((1, ROWS, width), lambda i, p: (p[n - 1 - i] % 2, 0, 0)))] * 2,
         ((length, width), bf16, row(width)),
-        ((8, HD), f32, whole((8, HD))),
+        ((8, width), f32, whole((8, width))),
         ((8, HD), f32, whole((8, HD))),
     ]
     return pl.pallas_call(
@@ -423,7 +485,7 @@
             num_scalar_prefetch=1,
             grid=(n,),
             in_specs=[
-                *[whole((ROWS, width))] * 4,
+                *[whole((ROWS, width))] * 8,
                 whole((width, nqkv)),
                 whole((width, nq), (0, nqkv // nq)),
                 whole((length, nqkv)),
@@ -433,11 +495,11 @@
                 row(nk),
                 row(HD),
                 row(HD),
-                whole((1, HD)),
-                whole((1, HD)),
+                whole((8, HD)),
             ],
             out_specs=[o[2] for o in out],
             scratch_shapes=[
+                pltpu.VMEM((ROWS, width), bf16),
                 pltpu.VMEM((ROWS, width), bf16),
                 pltpu.VMEM((nk // HD, length, HD), f32),
                 pltpu.VMEM((nk // HD, length, HD), f32),
@@ -448,65 +510,71 @@
         compiler_params=params(),
         cost_estimate=cost(9e9, 18e6, 3e6),
         name="backward_attention",
-    )(place, *branch, weights, weights, low, att, totals, qraw, kraw, cos, sin, qgain, kgain)
-
-
-def projection_weights_kernel(first, branch, grads, att, out):
+    )(place, *branch, *tokens, weights, weights, low, att, totals, qraw, kraw, cos, sin, head_gains)
+
+
+def projection_weights_kernel(per_device, first, branch, grads, att, gain, second_gain, heads, out):
     wide = grads.shape[1]
+    more = wide + att.shape[1]
     out[:, :wide] = t_matmul(first[...], grads[...]).astype(bf16)
-    out[:, wide:] = t_matmul(branch[...], att[...]).astype(bf16)
-
-
-def projection_weights(first, branch, grads, att):
+    out[:, wide:more] = t_matmul(branch[...], att[...]).astype(bf16)
+    rows = out.shape[0]
+    same = equal_iota(rows, rows, lambda r, c: r == c)
+    stands = of_head(rows, per_device, pl.program_id(0) * rows)
+    lane = lax.broadcasted_iota(jnp.int32, (rows, HD), 1)
+    columns = jnp.zeros((rows, HD), f32)
+    for k, (mask, values) in enumerate(
+        [(same, gain[:1, :]), (same, second_gain[:1, :]), (stands, heads[:1, :]), (stands, heads[1:2, :])]
+    ):
+        column = jnp.sum(jnp.where(mask, values, 0.0), axis=1, keepdims=True)
+        columns = jnp.where(lane == k, column, columns)
+    out[:, more:] = columns.astype(bf16)
+
+
+def projection_weights(first, branch, grads, att, gain, second_gain, heads):
     length, width = first.shape
     wide, nq = grads.shape[1], att.shape[1]
     return pl.pallas_call(
-        projection_weights_kernel,
+        functools.partial(projection_weights_kernel, width // lax.axis_size(FSDP)),
         grid=(width // 256,),
         in_specs=[
             pl.BlockSpec((length, 256), lambda i: (0, i)),
             pl.BlockSpec((length, 256), lambda i: (0, i)),
             whole((length, wide)),
             whole((length, nq)),
+            pl.BlockSpec((8, 256), lambda i: (0, i)),
+            pl.BlockSpec((8, 256), lambda i: (0, i)),
+            whole((8, HD)),
         ],
-        out_specs=pl.BlockSpec((256, wide + nq), lambda i: (i, 0)),
-        out_shape=jax.ShapeDtypeStruct((width, wide + nq), bf16),
+        out_specs=pl.BlockSpec((256, wide + nq + HD), lambda i: (i, 0)),
+        out_shape=jax.ShapeDtypeStruct((width, wide + nq + HD), bf16),
         compiler_params=params(),
         cost_estimate=cost(3.2e9, 10e6),
         name="projection_weights",
-    )(first, branch, grads, att)
-
-
-def tokens_back_kernel(tokens, mine, from_core, from_z, grad_middle, gain, grad_tokens, gain_part):
+    )(first, branch, grads, att, gain, second_gain, heads)
+
+
+def tokens_back_kernel(tokens, mine, from_core, from_z, grad_middle, gain, grad_tokens):
     u = mine[...].astype(f32) + from_core[...].astype(f32) + from_z[...].astype(f32)
-    grad, part = norm_back(tokens[...].astype(f32), gain[...], u)
+    grad, _ = norm_back(tokens[...].astype(f32), gain[:1, :], u)
     grad_tokens[...] = grad_middle[...] + grad
 
-    @pl.when(pl.program_id(0) == 0)
-    def _():
-        gain_part[...] = jnp.zeros_like(gain_part)
-
-    gain_part[:1, :] += part
-
-
-def tokens_back(tokens, part, from_core, from_z, grad_middle, gain):
+
+def tokens_back(tokens, mine, from_core, from_z, grad_middle, gain):
     width = tokens.shape[1]
     half = ROWS // 2
     row = pl.BlockSpec((half, width), lambda i: (i, 0))
-    first = pl.BlockSpec((None, None, half, width), lambda i: (0, 0, i, 0))
+    first = pl.BlockSpec((None, half, width), lambda i: (0, i, 0))
     return pl.pallas_call(
         tokens_back_kernel,
         grid=(2,),
-        in_specs=[row, first, pl.BlockSpec((None, half, width), lambda i: (0, i, 0)), row, row, whole((1, width))],
-        out_specs=[row, whole((8, width))],
-        out_shape=[
-            jax.ShapeDtypeStruct((ROWS, width), f32),
-            jax.ShapeDtypeStruct((8, width), f32),
-        ],
+        in_specs=[row, first, first, row, row, whole((8, width))],
+        out_specs=row,
+        out_shape=jax.ShapeDtypeStruct((ROWS, width), f32),
         compiler_params=params(),
         cost_estimate=cost(4e6, 4e6),
         name="tokens_back",
-    )(tokens, part, from_core, from_z, grad_middle, gain)
+    )(tokens, mine, from_core, from_z, grad_middle, gain)
 
 
 def swapped(value, axis):
@@ -518,11 +586,14 @@
     return [own, over_z, swapped(own, "core"), swapped(over_z, "core")]
 
 
-def tp_scatter(part):
-    part = part.reshape(2, 2, *part.shape[1:])
-    from_core = swapped(part[1], "core")
-    passed = (part[0, 1].astype(f32) + from_core[1].astype(f32)).astype(bf16)
-    return part, from_core, swapped(passed, "zl")
+def tp_scatter(mine, other):
+    from_core = swapped(other, "core")
+    passed = (mine[1].astype(f32) + from_core[1].astype(f32)).astype(bf16)
+    return mine, from_core, swapped(passed, "zl")
+
+
+def after(value, *others):
+    return lax.optimization_barrier((value, *others))[0]
 
 
 def from_everyone(shard, axes):
@@ -560,7 +631,6 @@
     down_weight,
     cotangent,
 ):
-    count = lax.axis_size(FSDP)
     width = tokens.shape[2]
     nq, nk = query_weight.shape[1], key_weight.shape[1]
     units = gate_weight.shape[1]
@@ -573,67 +643,64 @@
     place = place.astype(jnp.int32)
     cos, sin = rotary_tables(4 * ROWS)
 
-    gains = jnp.concatenate([attention_gain, feed_gain, query_gain, key_gain])
-    gains = jnp.pad(gains, (0, -gains.shape[0] % 128))[None]
-    gains = from_everyone(gains, FSDP)[:, 0].astype(f32)
     heads = query_gain.shape[0]
-    first_gain = gains[:, :rows].reshape(1, width)
-    second_gain = gains[:, rows : 2 * rows].reshape(1, width)
-    qgain = gains[:, 2 * rows : 2 * rows + heads].reshape(1, HD)
-    kgain = gains[:, 2 * rows + heads : 2 * rows + 2 * heads].reshape(1, HD)
-
-    weights = jnp.concatenate([query_weight, key_weight, value_weight, output_weight], axis=1)
+    tall = lambda v: jnp.pad(v, (0, rows - v.shape[0]))[:, None]
+    columns = [tall(v) for v in (attention_gain, feed_gain, query_gain, key_gain)]
+    weights = jnp.concatenate(
+        [query_weight, key_weight, value_weight, output_weight, *columns, jnp.zeros((rows, HD - 4), bf16)], axis=1
+    )
     weights = from_everyone(weights, FSDP).reshape(width, -1)
     feed = jnp.concatenate([gate_weight, up_weight, down_weight], axis=1)
     feed = lax.all_gather(feed, FSDP, axis=0, tiled=True)
-
     token_blocks = tp_gather(x)
-    grad_blocks = tp_gather(dy)
-
-    first, qraw, kraw, low, att, totals, part = forward_attention(
-        place, token_blocks, first_gain, qgain, kgain, weights, nq, nk, cos, sin
-    )
-    middle, second = middle_step(x, *tp_scatter(part), second_gain)
+    grad_blocks = tp_gather(after(dy, token_blocks[1]))
+
+    first, qraw, kraw, low, att, totals, mine, other, gains, head_gains = forward_attention(
+        place, token_blocks, weights, nq, nk, cos, sin
+    )
+    middle, second = middle_step(x, *tp_scatter(mine, other), gains)
     second_blocks = tp_gather(second)
-    hidden, grad_units, part = feed_step(second_blocks, grad_blocks, feed, units)
-    grad_middle, branch, feed_gain_part = middle_back(middle, *tp_scatter(part), dy, second_gain)
-    feed_sums = summed_rows(feed_weights(second_blocks, grad_blocks, grad_units, hidden))
-
-    mine, from_core, from_z = tp_scatter(feed_out(hidden, feed))
-    output = middle + mine[0, 0].astype(f32) + from_core[0].astype(f32) + from_z.astype(f32)
+    hidden, grad_units, mine, other = feed_step(second_blocks, grad_blocks, feed, units)
+    feed_grads = feed_weights(second_blocks, grad_blocks, grad_units, hidden)
+    mine, from_core, from_z = tp_scatter(mine, other)
+    grad_middle, branch, feed_gain_part = middle_back(
+        middle, mine, from_core, after(from_z, feed_grads), dy, gains
+    )
+    feed_sums = summed_rows(feed_grads)
+
+    branch_blocks = tp_gather(branch)
+    mine, from_core, from_z = tp_scatter(*feed_out(hidden, feed))
+    output = middle + mine[0].astype(f32) + from_core[0].astype(f32) + from_z.astype(f32)
     output = output.astype(bf16)
 
-    branch_blocks = tp_gather(branch)
-    grads, part, branch_rows, qpart, kpart = backward_attention(
-        place, branch_blocks, weights, low, att, totals, qraw, kraw, cos, sin, qgain, kgain
-    )
-    sums = summed_rows(projection_weights(first, branch_rows, grads, att))
-    tokens_grad, first_gain_part = tokens_back(x, *tp_scatter(part), grad_middle, first_gain)
-
-    gain_parts = jnp.concatenate(
-        [
-            first_gain_part[0].reshape(count, rows),
-            feed_gain_part[0].reshape(count, rows),
-            qpart[0].reshape(count, heads),
-            kpart[0].reshape(count, heads),
-        ],
-        axis=1,
-    )
-    gain_parts = jnp.pad(gain_parts, ((0, 0), (0, -gain_parts.shape[1] % 128)))
-    gain_parts = jnp.repeat(gain_parts, 4, axis=0)[:, None, :]
-    gain_sums = jnp.sum(lax.all_to_all(gain_parts, EVERY, 0, 0, tiled=True), axis=(0, 1))
+    branch_blocks[3] = after(branch_blocks[3], from_core)
+    grads, mine, other, branch_rows, gain_part, head_part = backward_attention(
+        place, branch_blocks, token_blocks, weights, low, att, totals, qraw, kraw, cos, sin, head_gains
+    )
+    projection_grads = projection_weights(
+        first, branch_rows, grads, att, gain_part, feed_gain_part, head_part
+    )
+    mine, from_core, from_z = tp_scatter(mine, other)
+    tokens_grad = tokens_back(
+        x, mine, from_core, after(from_z, projection_grads, feed_sums, output), grad_middle, gains
+    )
+    sums = summed_rows(projection_grads)
+
+    gain_sums = sums[:, nq + 2 * nk + nq :]
+    over_z = swapped(gain_sums, "zl")
+    gain_sums = gain_sums + over_z + (swapped(gain_sums, "core") + swapped(over_z, "core"))
 
     return (
         output[None],
         tokens_grad[None],
-        gain_sums[:rows],
+        gain_sums[:, 0],
         sums[:, :nq],
         sums[:, nq : nq + nk],
         sums[:, nq + nk : nq + 2 * nk],
-        gain_sums[2 * rows : 2 * rows + heads],
-        gain_sums[2 * rows + heads : 2 * rows + 2 * heads],
-        sums[:, nq + 2 * nk :],
-        gain_sums[rows : 2 * rows],
+        gain_sums[:heads, 2],
+        gain_sums[:heads, 3],
+        sums[:, nq + 2 * nk : nq + 2 * nk + nq],
+        gain_sums[:, 1],
         feed_sums[:, :units],
         feed_sums[:, units : 2 * units],
         feed_sums[:, 2 * units :],

time: 441 us -> 401 us (0.909)
  starting transfers between devices: 69.2 us -> 41.8 us
  local copies, waits for them, and re-layouts: 23.6 us -> 15.2 us
  Pallas kernels: 96.8 us -> 102 us
    ppermute x20 -> x23, waiting for transfers between devices: 164 us -> 211 us  [swapped(): return lax.ppermute(value, axis, [(0, 1), (1, 0)])]
    all_to_all x2, waiting for transfers between devices: 45.5 us -> 0.01 us  [summed_rows(): parts = lax.all_to_all(blocks, FSDP, 0, 0, tiled=True)]
    all_to_all x2, starting transfers between devices: 31 us -> 20.4 us  [summed_rows(): parts = lax.all_to_all(blocks, FSDP, 0, 0, tiled=True)]
    all_to_all x1 -> x0, starting transfers between devices: 10 us -> none  [local(): lax.all_to_all(gain_parts, EVERY, 0, 0, tiled=True)]
    slice x13 -> x4, local copies, waits for them, and re-layouts: 11.1 us -> 2.09 us  [the longest x1 0.73 us: local(): gain_sums[:heads, 3]]
    all_to_all x2 -> x1, starting transfers between devices: 18.3 us -> 10.6 us  [from_everyone(): return lax.all_to_all(copies, axes, split_axis=0, concat_axis=0, tiled=True)]
    all_to_all x2 -> x1, waiting for transfers between devices: 5.24 us -> 0.01 us  [from_everyone(): return lax.all_to_all(copies, axes, split_axis=0, concat_axis=0, tiled=True)]
    ppermute x20 -> x23, starting transfers between devices: 9.9 us -> 10.8 us  [swapped(): return lax.ppermute(value, axis, [(0, 1), (1, 0)])]
  transfers between devices with their start and end apart: 26 -> 27, of which waited for: 15 -> 16; matrix products, arithmetic and copies ran while one was open for 6% -> 5% of each run, Pallas kernels for 11% -> 19%
where the time goes in v2:
time: 401 us; the launch traced here: 399 us
  waiting for transfers between devices  211 us (53%)
  Pallas kernels  102 us (25%)
  starting transfers between devices  41.8 us (10%)
  local copies, waits for them, and re-layouts  15.2 us (4%)
  other arithmetic  14.9 us (4%)
  between operations  14.3 us (4%)
    ppermute x23, waiting for transfers between devices, swapped(): return lax.ppermute(value, axis, [(0, 1), (1, 0)])  211 us
    pallas_call x1, Pallas kernels, backward_attention(): pl.pallas_call(backward_attention_kernel, grid_spec=pltpu.PrefetchScalarG...  28.8 us
    pallas_call x1, Pallas kernels, forward_attention(): pl.pallas_call(functools.partial(forward_attention_kernel, width // lax.a...  23.1 us
    all_to_all x2, starting transfers between devices, summed_rows(): parts = lax.all_to_all(blocks, FSDP, 0, 0, tiled=True)  20.4 us
    pallas_call x1, Pallas kernels, feed_step(): pl.pallas_call(feed_kernel, grid=(4,), in_specs=[*[whole((ROWS, width))]...  17.7 us
    ppermute x23, starting transfers between devices, swapped(): return lax.ppermute(value, axis, [(0, 1), (1, 0)])  10.8 us
    all_to_all x1, starting transfers between devices, from_everyone(): return lax.all_to_all(copies, axes, split_axis=0, concat_axis=0, tiled=True)  10.6 us
    pallas_call x1, Pallas kernels, feed_weights(): pl.pallas_call(feed_weights_kernel, grid=(width // 256,), in_specs=[*[pl....  10 us
  transfers between devices with their start and end apart: 27, of which 16 were waited for; matrix products, arithmetic and copies ran while one was open for 5% of the time, Pallas kernels for 19%

profile of v2, /device:TPU:28, one launch (start us, length us, event | category | flops | bytes accessed | tf_op | source)
XLA Modules:
  0.0 399.1 jit_solution(17614717289639349169)
XLA Ops:
  12.7 1.9 broadcast_in_dim.31
  14.6 10.6 %all-to-all-start = ((bf16[32,32,1664]{2,1,0:T(8,128)(2,1)}), bf16[32,32,1664]{2,1,0:T(8,128)(2,1)S(1)}, u32[]{:S(2)}, u32[]{:S(2)}) async-start(bf16[32,32,1664]{2,1,0:T(8,128)(2,1)} %broadcast_in_dim.31), calls=%async_computation | async-start | bytes 6815744 | tf_op jit(solution)/shard_map/all_to_all | solution.py:601
  26.3 49.0 %collective-permute-done.refs_1_.refs_5_ = bf16[256,1024]{1,0:T(8,128)(2,1)} collective-permute-done((bf16[256,1024]{1,0:T(8,128)(2,1)}, bf16[256,1024]{1,0:T(8,128)(2,1)}, u32[]{:S(2)}, u32[]{:S(2)}) %collective-permute-start) | collective-permute-done | bytes 524320 | tf_op jit(solution)/shard_map/ppermute | solution.py:581
  75.8 2.0 fusion.8
  79.1 1.8 copy-done
  80.9 23.1 %forward_attention.1 = (bf16[1024,1024]{1,0:T(8,128)(2,1)}, f32[1024,512]{1,0:T(8,128)}, f32[1024,256]{1,0:T(8,128)}, bf16[1024,1024]{1,0:T(8,128)(2,1)}, bf16[1...) custom-call(s32[4]{0:T(128)} %fusion.11.place, ...), custom_call_target="tpu_custom_call" | custom-call | flops 875000000 | bytes 2000000 | tf_op jit(solution)/shard_map/forward_attention/pallas_call | solution.py:204
  104.6 2.5 collective-permute-done.3.from_core
  107.1 1.6 fusion.2
  110.8 15.6 %collective-permute-done.4.from_z = bf16[256,1024]{1,0:T(8,128)(2,1)S(1)} collective-permute-done((bf16[256,1024]{1,0:T(8,128)(2,1)S(1)}, bf16[256,1024]{1,0:T(8,128)(2,1)S(1)}, u32[]{:S(2)}, u32[]{:S(2)}) %collective-permute-start.4) | collective-permute-done | bytes 524320 | tf_op jit(solution)/shard_map/ppermute | solution.py:581
  127.2 2.6 middle_step.1
  130.2 7.4 %collective-permute-done.8.refs_5_ = bf16[256,1024]{1,0:T(8,128)(2,1)S(1)} collective-permute-done((bf16[256,1024]{1,0:T(8,128)(2,1)S(1)}, bf16[256,1024]{1,0:T(8,128)(2,1)S(1)}, u32[]{:S(2)}, u32[]{:S(2)}) %collective-permute-start.8) | collective-permute-done | bytes 524320 | tf_op jit(solution)/shard_map/ppermute | solution.py:581
  138.2 10.5 %collective-permute-done.5.refs_1_ = bf16[256,1024]{1,0:T(8,128)(2,1)S(1)} collective-permute-done((bf16[256,1024]{1,0:T(8,128)(2,1)}, bf16[256,1024]{1,0:T(8,128)(2,1)S(1)}, u32[]{:S(2)}, u32[]{:S(2)}) %collective-permute-start.5) | collective-permute-done | bytes 524320 | tf_op jit(solution)/shard_map/ppermute | solution.py:581
  148.7 1.9 collective-permute-done.7.refs_3_
  151.5 17.7 %feed_step.1 = (bf16[1024,768]{1,0:T(8,128)(2,1)}, bf16[1024,1536]{1,0:T(8,128)(2,1)}, bf16[2,256,1024]{2,1,0:T(8,128)(2,1)}, bf16[2,256,1024]{2,1,0:T(8,128)(2,1)}) custom-call(bf16[256,1024]{1,0:T(8,128)(2,1)} %get-tuple-element.48.refs_0_, bf16[256,1024]{1,0:T(8,128)(2,1)} %copy-done.8, bf16[256,1024]{1,0:T(8,128)(2,1)} %copy-done.11, ...), custom_call_target="tpu_custom_call" | custom-call | flops 1000000000 | bytes 2000000 | tf_op jit(solution)/shard_map/feed_step/pallas_call | solution.py:283
  169.1 10.0 %feed_weights.1 = bf16[1024,2304]{1,0:T(8,128)(2,1)} custom-call(bf16[256,1024]{1,0:T(8,128)(2,1)} %get-tuple-element.48.refs_0_, bf16[256,1024]{1,0:T(8,128)(2,1)} %copy-done.8, bf16[256,1024]{1,0:T(8,128)(2,1)} %copy-done.11, bf16[256,1024]{1,0:T(8,128)(2,1)} %copy-done.12, bf16[256,1024]{1,0:T(8,128)(2,1)} %bitcast.43, bf16[256,1024]{1,0:T(8,128)(2,1)} %copy-done.7, ...), custom_call_target="tpu_custom_call" | custom-call | flops 600000000 | bytes 1750000 | tf_op jit(solution)/shard_map/feed_weights/pallas_call | solution.py:344
  179.1 9.8 %all-to-all-start.1 = ((bf16[32,32,2304]{2,1,0:T(8,128)(2,1)}), bf16[32,32,2304]{2,1,0:T(8,128)(2,1)}, u32[]{:S(2)}, u32[]{:S(2)}) async-start(bf16[32,32,2304]{2,1,0:T(8,128)(2,1)} %bitcast.34), calls=%async_computation.1 | async-start | bytes 9437184 | tf_op jit(solution)/shard_map/all_to_all | solution.py:607
  189.0 2.6 collective-permute-done.13.from_core
  192.1 5.7 %feed_out.1 = (bf16[2,256,1024]{2,1,0:T(8,128)(2,1)}, bf16[2,256,1024]{2,1,0:T(8,128)(2,1)}) custom-call(bf16[1024,768]{1,0:T(8,128)(2,1)} %get-tuple-element.50.hidden.refs_9_, bf16[1024,2304]{1,0:T(8,128)(2,1)} %all-gather.2.cloned.1.call-done.refs_8_.refs_9_.refs_10_.wd), custom_call_target="tpu_custom_call" | custom-call | flops 200000000 | bytes 625000 | tf_op jit(solution)/shard_map/feed_out/pallas_call | solution.py:312
  197.9 53.4 %collective-permute-done.14.from_z = bf16[256,1024]{1,0:T(8,128)(2,1)S(1)} collective-permute-done((bf16[256,1024]{1,0:T(8,128)(2,1)S(1)}, bf16[256,1024]{1,0:T(8,128)(2,1)S(1)}, u32[]{:S(2)}, u32[]{:S(2)}) %collective-permute-start.14) | collective-permute-done | bytes 524320 | tf_op jit(solution)/shard_map/ppermute | solution.py:581
  252.2 3.1 middle_back.1
  255.3 1.9 collective-permute-start.15
  257.2 12.0 %collective-permute-done.15.refs_1_ = bf16[256,1024]{1,0:T(8,128)(2,1)S(1)} collective-permute-done((bf16[256,1024]{1,0:T(8,128)(2,1)}, bf16[256,1024]{1,0:T(8,128)(2,1)S(1)}, u32[]{:S(2)}, u32[]{:S(2)}) %collective-permute-start.15) | collective-permute-done | bytes 524320 | tf_op jit(solution)/shard_map/ppermute | solution.py:581
  269.8 2.1 collective-permute-done.17.refs_3_
  272.9 28.8 %backward_attention.1 = (bf16[1024,1024]{1,0:T(8,128)(2,1)}, bf16[2,256,1024]{2,1,0:T(8,128)(2,1)}, bf16[2,256,1024]{2,1,0:T(8,128)(2,1)}, bf16[1024,1024]{1,0:T...) custom-call(s32[4]{0:T(128)} %fusion.11.place, bf16[256,1024]{1,0:T(8,128)(2,1)} %get-tuple-element.57.refs_0_, ...), custom_call_target="tpu_custom_call" | custom-call | flops 1124999936 | bytes 2250000 | tf_op jit(solution)/shard_map/backward_attention/pallas_call | solution.py:482
  301.7 8.2 %projection_weights.1 = bf16[1024,1664]{1,0:T(8,128)(2,1)} custom-call(bf16[1024,1024]{1,0:T(8,128)(2,1)} %get-tuple-element.67.first, bf16[1024,1024]{1,0:T(8,128)(2,1)} %get-tuple-element.68.branch, bf16[1024,1024]{1,0:T(8,128)(2,1)} %get-tuple-element.69.grads, bf16[1024,512]{1,0:T(8,128)(2,1)} %get-tuple-element.60.refs_11_.att, ...), custom_call_target="tpu_custom_call" | custom-call | flops 400000000 | bytes 1250000 | tf_op jit(solution)/shard_map/projection_weights/pallas_call | solution.py:537
  309.9 10.6 %all-to-all-start.2 = ((bf16[32,32,1664]{2,1,0:T(8,128)(2,1)}), bf16[32,32,1664]{2,1,0:T(8,128)(2,1)S(1)}, u32[]{:S(2)}, u32[]{:S(2)}) async-start(bf16[32,32,1664]{2,1,0:T(8,128)(2,1)} %bitcast.35), calls=%async_computation.2 | async-start | bytes 6815744 | tf_op jit(solution)/shard_map/all_to_all | solution.py:607
  323.5 1.6 fusion.5
  326.0 43.9 %collective-permute-done.12 = bf16[256,1024]{1,0:T(8,128)(2,1)S(1)} collective-permute-done((bf16[256,1024]{1,0:T(8,128)(2,1)S(1)}, bf16[256,1024]{1,0:T(8,128)(2,1)S(1)}, u32[]{:S(2)}, u32[]{:S(2)}) %collective-permute-start.12) | collective-permute-done | bytes 524320 | tf_op jit(solution)/shard_map/ppermute | solution.py:581
  371.1 3.0 convert_reduce_fusion
  374.1 6.7 %collective-permute-done.19.from_z = bf16[256,1024]{1,0:T(8,128)(2,1)S(1)} collective-permute-done((bf16[256,1024]{1,0:T(8,128)(2,1)S(1)}, bf16[256,1024]{1,0:T(8,128)(2,1)S(1)}, u32[]{:S(2)}, u32[]{:S(2)}) %collective-permute-start.19) | collective-permute-done | bytes 524320 | tf_op jit(solution)/shard_map/ppermute | solution.py:581
  381.6 2.9 tokens_back.1
  387.9 1.8 collective-permute-done.20
  (106 shorter events, 28.4 us)
Async XLA Ops:
  7.2 143.4 %all-gather.2.cloned.1.call-start = ((), (), s32[]{:S(2)}) async-start(), calls=%async_computation.3 | async-start | bytes 4866048 | tf_op jit(solution)/shard_map/all_gather | solution.py:654
  14.6 64.5 %all-to-all-start = ((bf16[32,32,1664]{2,1,0:T(8,128)(2,1)}), bf16[32,32,1664]{2,1,0:T(8,128)(2,1)S(1)}, u32[]{:S(2)}, u32[]{:S(2)}) async-start(bf16[32,32,1664]{2,1,0:T(8,128)(2,1)} %broadcast_in_dim.31), calls=%async_computation | async-start | bytes 6815744 | tf_op jit(solution)/shard_map/all_to_all | solution.py:601
  25.2 50.1 %collective-permute-start = (bf16[256,1024]{1,0:T(8,128)(2,1)}, bf16[256,1024]{1,0:T(8,128)(2,1)}, u32[]{:S(2)}, u32[]{:S(2)}) collective-permute-start(bf16[256,1024]{1,0:T(8,128)(2,1)} %bitcast.36), channel_id=1, source_target_pairs={{0,2},{2,0},{1,3},{3,1},{4,6},{6,4},{5,7},{7,5},{8,10},{10,8},{9,1... | collective-permute-start | bytes 1572872 | tf_op jit(solution)/shard_map/ppermute | solution.py:581
  26.3 52.8 %collective-permute-start.1 = (bf16[256,1024]{1,0:T(8,128)(2,1)}, bf16[256,1024]{1,0:T(8,128)(2,1)}, u32[]{:S(2)}, u32[]{:S(2)}) collective-permute-start(bf16[256,1024]{1,0:T(8,128)(2,1)} %bitcast.37), channel_id=1, source_target_pairs={{0,1},{1,0},{2,3},{3,2},{4,5},{5,4},{6,7},{7,6},{8,9},{9,8},{10,11... | collective-permute-start | bytes 1572872 | tf_op jit(solution)/shard_map/ppermute | solution.py:581
  75.3 3.8 collective-permute-start.2
  104.0 3.1 collective-permute-start.3
  108.7 17.8 %collective-permute-start.4 = (bf16[256,1024]{1,0:T(8,128)(2,1)S(1)}, bf16[256,1024]{1,0:T(8,128)(2,1)S(1)}, u32[]{:S(2)}, u32[]{:S(2)}) collective-permute-start(bf16[256,1024]{1,0:T(8,128)(2,1)S(1)} %fusion.2), channel_id=1, source_target_pairs={{0,2},{2,0},{1,3},{3,1},{4,6},{6,4},{5,7},{7,5},{8,10},{10,8},{9,1... | collective-permute-start | bytes 1572872 | tf_op jit(solution)/shard_map/ppermute | solution.py:581
  109.2 28.4 %collective-permute-start.8 = (bf16[256,1024]{1,0:T(8,128)(2,1)S(1)}, bf16[256,1024]{1,0:T(8,128)(2,1)S(1)}, u32[]{:S(2)}, u32[]{:S(2)}) collective-permute-start(bf16[256,1024]{1,0:T(8,128)(2,1)S(1)} %bitcast.45), channel_id=1, source_target_pairs={{0,2},{2,0},{1,3},{3,1},{4,6},{6,4},{5,7},{7,5},{8,10},{10,8},{9,1... | collective-permute-start | bytes 1572872 | tf_op jit(solution)/shard_map/ppermute | solution.py:581
  129.8 18.9 %collective-permute-start.5 = (bf16[256,1024]{1,0:T(8,128)(2,1)}, bf16[256,1024]{1,0:T(8,128)(2,1)S(1)}, u32[]{:S(2)}, u32[]{:S(2)}) collective-permute-start(bf16[256,1024]{1,0:T(8,128)(2,1)} %get-tuple-element.48.refs_0_), channel_id=1, source_target_pairs={{0,2},{2,0},{1,3},{3,1},{4,6},{6,4},{5,7},{7,5},{8,10},{10,8},{9,1... | collective-permute-start | bytes 1572872 | tf_op jit(solution)/shard_map/ppermute | solution.py:581
  130.2 18.5 %collective-permute-start.9 = (bf16[256,1024]{1,0:T(8,128)(2,1)S(1)}, bf16[256,1024]{1,0:T(8,128)(2,1)S(1)}, u32[]{:S(2)}, u32[]{:S(2)}) collective-permute-start(bf16[256,1024]{1,0:T(8,128)(2,1)S(1)} %bitcast.46), channel_id=1, source_target_pairs={{0,1},{1,0},{2,3},{3,2},{4,5},{5,4},{6,7},{7,6},{8,9},{9,8},{10,11... | collective-permute-start | bytes 1572872 | tf_op jit(solution)/shard_map/ppermute | solution.py:581
  137.6 11.1 %collective-permute-start.10 = (bf16[256,1024]{1,0:T(8,128)(2,1)S(1)}, bf16[256,1024]{1,0:T(8,128)(2,1)S(1)}, u32[]{:S(2)}, u32[]{:S(2)}) collective-permute-start(bf16[256,1024]{1,0:T(8,128)(2,1)S(1)} %collective-permute-done.8.refs_5_), channel_id=1, source_target_pairs={{0,1},{1,0},{2,3},{3,2},{4,5},{5,4},{6,7},{7,6},{8,9},{9,8},{10,11... | collective-permute-start | bytes 1572872 | tf_op jit(solution)/shard_map/ppermute | solution.py:581
  137.7 11.1 %collective-permute-start.6 = (bf16[256,1024]{1,0:T(8,128)(2,1)}, bf16[256,1024]{1,0:T(8,128)(2,1)S(1)}, u32[]{:S(2)}, u32[]{:S(2)}) collective-permute-start(bf16[256,1024]{1,0:T(8,128)(2,1)} %get-tuple-element.48.refs_0_), channel_id=1, source_target_pairs={{0,1},{1,0},{2,3},{3,2},{4,5},{5,4},{6,7},{7,6},{8,9},{9,8},{10,11... | collective-permute-start | bytes 1572872 | tf_op jit(solution)/shard_map/ppermute | solution.py:581
  148.7 1.9 collective-permute-start.7
  179.1 130.7 %all-to-all-start.1 = ((bf16[32,32,2304]{2,1,0:T(8,128)(2,1)}), bf16[32,32,2304]{2,1,0:T(8,128)(2,1)}, u32[]{:S(2)}, u32[]{:S(2)}) async-start(bf16[32,32,2304]{2,1,0:T(8,128)(2,1)} %bitcast.34), calls=%async_computation.1 | async-start | bytes 9437184 | tf_op jit(solution)/shard_map/all_to_all | solution.py:607
  188.9 2.7 collective-permute-start.13
  191.9 59.5 %collective-permute-start.14 = (bf16[256,1024]{1,0:T(8,128)(2,1)S(1)}, bf16[256,1024]{1,0:T(8,128)(2,1)S(1)}, u32[]{:S(2)}, u32[]{:S(2)}) collective-permute-start(bf16[256,1024]{1,0:T(8,128)(2,1)S(1)} %fusion.4), channel_id=1, source_target_pairs={{0,2},{2,0},{1,3},{3,1},{4,6},{6,4},{5,7},{7,5},{8,10},{10,8},{9,1... | collective-permute-start | bytes 1572872 | tf_op jit(solution)/shard_map/ppermute | solution.py:581
  197.9 71.9 %collective-permute-start.11 = (bf16[2,256,1024]{2,1,0:T(8,128)(2,1)}, bf16[2,256,1024]{2,1,0:T(8,128)(2,1)S(1)}, u32[]{:S(2)}, u32[]{:S(2)}) collective-permute-start(bf16[2,256,1024]{2,1,0:T(8,128)(2,1)} %get-tuple-element.52), channel_id=1, source_target_pairs={{0,1},{1,0},{2,3},{3,2},{4,5},{5,4},{6,7},{7,6},{8,9},{9,8},{10,11... | collective-permute-start | bytes 3145736 | tf_op jit(solution)/shard_map/ppermute | solution.py:581
  255.3 14.0 %collective-permute-start.15 = (bf16[256,1024]{1,0:T(8,128)(2,1)}, bf16[256,1024]{1,0:T(8,128)(2,1)S(1)}, u32[]{:S(2)}, u32[]{:S(2)}) collective-permute-start(bf16[256,1024]{1,0:T(8,128)(2,1)} %get-tuple-element.57.refs_0_), channel_id=1, source_target_pairs={{0,2},{2,0},{1,3},{3,1},{4,6},{6,4},{5,7},{7,5},{8,10},{10,8},{9,1... | collective-permute-start | bytes 1572872 | tf_op jit(solution)/shard_map/ppermute | solution.py:581
  269.2 2.6 collective-permute-start.17
  269.2 2.9 collective-permute-start.16
  269.8 31.9 %copy-start.14 = (bf16[2,256,1024]{2,1,0:T(8,128)(2,1)}, bf16[2,256,1024]{2,1,0:T(8,128)(2,1)S(1)}, u32[]{:S(2)}) copy-start(bf16[2,256,1024]{2,1,0:T(8,128)(2,1)S(1)} %collective-permute-done.11) | copy-start | bytes 3145732
  309.9 75.3 %all-to-all-start.2 = ((bf16[32,32,1664]{2,1,0:T(8,128)(2,1)}), bf16[32,32,1664]{2,1,0:T(8,128)(2,1)S(1)}, u32[]{:S(2)}, u32[]{:S(2)}) async-start(bf16[32,32,1664]{2,1,0:T(8,128)(2,1)} %bitcast.35), calls=%async_computation.2 | async-start | bytes 6815744 | tf_op jit(solution)/shard_map/all_to_all | solution.py:607
  320.5 49.4 %copy-start.2 = (f32[256,1024]{1,0:T(8,128)S(1)}, f32[256,1024]{1,0:T(8,128)}, u32[]{:S(2)}) copy-start(f32[256,1024]{1,0:T(8,128)} %get-tuple-element.47.middle) | copy-start | bytes 3145732
  320.5 49.4 %copy-start.13 = (bf16[2,256,1024]{2,1,0:T(8,128)(2,1)S(1)}, bf16[2,256,1024]{2,1,0:T(8,128)(2,1)}, u32[]{:S(2)}) copy-start(bf16[2,256,1024]{2,1,0:T(8,128)(2,1)} %get-tuple-element.51) | copy-start | bytes 3145732
  320.6 49.4 %copy-start.15 = (bf16[2,256,1024]{2,1,0:T(8,128)(2,1)S(1)}, bf16[2,256,1024]{2,1,0:T(8,128)(2,1)}, u32[]{:S(2)}) copy-start(bf16[2,256,1024]{2,1,0:T(8,128)(2,1)} %copy-done.14) | copy-start | bytes 3145732
  320.6 3.0 collective-permute-start.18
  322.2 47.7 %collective-permute-start.12 = (bf16[256,1024]{1,0:T(8,128)(2,1)S(1)}, bf16[256,1024]{1,0:T(8,128)(2,1)S(1)}, u32[]{:S(2)}, u32[]{:S(2)}) collective-permute-start(bf16[256,1024]{1,0:T(8,128)(2,1)S(1)} %fusion.3), channel_id=1, source_target_pairs={{0,2},{2,0},{1,3},{3,1},{4,6},{6,4},{5,7},{7,5},{8,10},{10,8},{9,1... | collective-permute-start | bytes 1572872 | tf_op jit(solution)/shard_map/ppermute | solution.py:581
  323.5 50.6 %copy-start.3 = (bf16[2,256,1024]{2,1,0:T(8,128)(2,1)}, bf16[2,256,1024]{2,1,0:T(8,128)(2,1)S(1)}, u32[]{:S(2)}) copy-start(bf16[2,256,1024]{2,1,0:T(8,128)(2,1)S(1)} %collective-permute-done.18.from_core) | copy-start | bytes 3145732
  325.1 55.7 %collective-permute-start.19 = (bf16[256,1024]{1,0:T(8,128)(2,1)S(1)}, bf16[256,1024]{1,0:T(8,128)(2,1)S(1)}, u32[]{:S(2)}, u32[]{:S(2)}) collective-permute-start(bf16[256,1024]{1,0:T(8,128)(2,1)S(1)} %fusion.5), channel_id=1, source_target_pairs={{0,2},{2,0},{1,3},{3,1},{4,6},{6,4},{5,7},{7,5},{8,10},{10,8},{9,1... | collective-permute-start | bytes 1572872 | tf_op jit(solution)/shard_map/ppermute | solution.py:581
  385.7 4.5 %collective-permute-start.21 = (f32[32,128]{1,0:T(8,128)S(1)}, f32[32,128]{1,0:T(8,128)S(1)}, u32[]{:S(2)}, u32[]{:S(2)}) collective-permute-start(f32[32,128]{1,0:T(8,128)S(1)} %slice.93), channel_id=1, source_target_pairs={{0,1},{1,0},{2,3},{3,2},{4,5},{5,4},{6,7},{7,6},{8,9},{9,8},{10,11... | collective-permute-start | bytes 49160 | tf_op jit(solution)/shard_map/ppermute | solution.py:581
  385.8 3.8 collective-permute-start.20
  389.7 1.2 collective-permute-start.22
  (18 other events, 106.3 us)
Sparse Core Ops, SparseCore 0:
  11.0 118.0 all-gather.1

commit v3 on v2

--- a/solution.py
+++ b/solution.py
@@ -3,6 +3,7 @@
 
 import jax
 import jax.numpy as jnp
+import numpy as np
 from jax import lax
 from jax.experimental import pallas as pl
 from jax.experimental.pallas import tpu as pltpu
@@ -17,6 +18,7 @@
 score_scale = 1.0 / math.sqrt(HD)
 log2_scale = score_scale / math.log(2.0)
 FSDP = ("x", "y", "zh")
+PLANE = ("x", "y")
 EVERY = ("x", "y", "zh", "zl", "core")
 f32 = jnp.float32
 bf16 = jnp.bfloat16
@@ -577,43 +579,112 @@
     )(tokens, mine, from_core, from_z, grad_middle, gain)
 
 
+def pack(first, second, gains, rows, heads):
+    widths = [a.shape[1] for a in first], [a.shape[1] for a in second]
+    split = sum(widths[0])
+
+    def kernel(gains, *refs):
+        out = refs[-1]
+        at = 0
+        for k, ref in enumerate(refs[:-1]):
+            at += HD * (k == len(first))
+            out[:, at : at + ref.shape[1]] = ref[...]
+            at += ref.shape[1]
+        g = gains[...].astype(f32)
+        lane = lax.broadcasted_iota(jnp.int32, (rows, HD), 1)
+        line = lax.broadcasted_iota(jnp.int32, (rows, HD), 0)
+        columns = jnp.zeros((rows, HD), f32)
+        places = [(0, rows), (rows, rows), (2 * rows, heads), (2 * rows + heads, heads)]
+        for k, (start, count) in enumerate(places):
+            mask = (lane == line + start) & (line < count)
+            column = jnp.sum(jnp.where(mask, g, 0.0), axis=1, keepdims=True)
+            columns = jnp.where(lane == k, column, columns)
+        out[:, split : split + HD] = columns.astype(bf16)
+
+    return pl.pallas_call(
+        kernel,
+        out_shape=jax.ShapeDtypeStruct((rows, split + HD + sum(widths[1])), bf16),
+        compiler_params=params(),
+        cost_estimate=cost(1e3, 5e5),
+        name="pack",
+    )(gains, *first, *second)
+
+
+def spread(zh, shard, other, split, planes):
+    rows, wide = shard.shape
+
+    def kernel(zh, shard, other, copies, rest, block, semaphores):
+        places = [pl.ds(pl.multiple_of((zh[0] ^ k) * rows, rows), rows) for k in range(2)]
+        for at, ref in zip(places, (shard, other)):
+            block[at, :] = ref[:, :split]
+        sent = [pltpu.make_async_copy(block, copies.at[k], semaphores.at[k]) for k in range(planes)]
+        for copy in sent:
+            copy.start()
+        for at, ref in zip(places, (shard, other)):
+            rest[at, :] = ref[:, split:]
+        for copy in sent:
+            copy.wait()
+
+    return pl.pallas_call(
+        kernel,
+        grid_spec=pltpu.PrefetchScalarGridSpec(
+            num_scalar_prefetch=1,
+            grid=(1,),
+            in_specs=[whole((rows, wide))] * 2,
+            out_specs=[pl.BlockSpec(memory_space=pl.ANY), whole((2 * rows, wide - split))],
+            scratch_shapes=[pltpu.VMEM((2 * rows, split), bf16), pltpu.SemaphoreType.DMA((planes,))],
+        ),
+        out_shape=[
+            jax.ShapeDtypeStruct((planes, 2 * rows, split), bf16),
+            jax.ShapeDtypeStruct((2 * rows, wide - split), bf16),
+        ],
+        compiler_params=params(),
+        cost_estimate=cost(1e3, 5e6),
+        name="spread",
+    )(zh, shard, other)
+
+
 def swapped(value, axis):
     return lax.ppermute(value, axis, [(0, 1), (1, 0)])
 
 
-def tp_gather(own):
-    over_z = swapped(own, "zl")
+def tp_gather(own, over_z=None):
+    over_z = swapped(own, "zl") if over_z is None else over_z
     return [own, over_z, swapped(own, "core"), swapped(over_z, "core")]
 
 
 def tp_scatter(mine, other):
     from_core = swapped(other, "core")
     passed = (mine[1].astype(f32) + from_core[1].astype(f32)).astype(bf16)
-    return mine, from_core, swapped(passed, "zl")
+    return mine, from_core, swapped(passed, "zl"), passed
 
 
 def after(value, *others):
     return lax.optimization_barrier((value, *others))[0]
 
 
-def from_everyone(shard, axes):
-    copies = jnp.broadcast_to(shard, (lax.axis_size(axes), *shard.shape))
-    return lax.all_to_all(copies, axes, split_axis=0, concat_axis=0, tiled=True)
-
-
-def summed_rows(part):
-    count = lax.axis_size(FSDP)
-    blocks = part.reshape(count, part.shape[0] // count, part.shape[1])
-    parts = lax.all_to_all(blocks, FSDP, 0, 0, tiled=True)
-    return jnp.sum(parts.astype(f32), axis=0)
+def sent_rows(part):
+    planes = lax.axis_size(PLANE)
+    rows, wide = part.shape[0] // (2 * planes), part.shape[1]
+    blocks = part.reshape(planes, 2 * rows, wide)
+    return lax.all_to_all(blocks, PLANE, 0, 0, tiled=True).reshape(planes, 2, rows, wide)
+
+
+def summed_rows(parts):
+    zh = lax.axis_index("zh")
+    half = lambda which: jnp.sum(
+        lax.dynamic_index_in_dim(parts, which, 1, keepdims=False).astype(f32), axis=0
+    )
+    return half(zh) + swapped(half(1 - zh).astype(bf16), "zh").astype(f32)
 
 
 def rotary_tables(length):
     midway = HD // 2
-    frequency = 1.0 / rope_base ** (jnp.arange(midway, dtype=f32) * 2.0 / HD)
-    angles = jnp.arange(length, dtype=f32)[:, None] * frequency[None, :]
-    cos, sin = jnp.cos(angles), jnp.sin(angles)
-    return jnp.concatenate([cos, cos], axis=1), jnp.concatenate([-sin, sin], axis=1)
+    frequency = 1.0 / rope_base ** (np.arange(midway) * 2.0 / HD)
+    angles = np.arange(length)[:, None] * frequency[None, :]
+    cos, sin = np.cos(angles), np.sin(angles)
+    tables = np.concatenate([cos, cos], axis=1), np.concatenate([-sin, sin], axis=1)
+    return [jnp.asarray(t.astype(np.float32)) for t in tables]
 
 
 def local(
@@ -644,47 +715,59 @@
     cos, sin = rotary_tables(4 * ROWS)
 
     heads = query_gain.shape[0]
-    tall = lambda v: jnp.pad(v, (0, rows - v.shape[0]))[:, None]
-    columns = [tall(v) for v in (attention_gain, feed_gain, query_gain, key_gain)]
-    weights = jnp.concatenate(
-        [query_weight, key_weight, value_weight, output_weight, *columns, jnp.zeros((rows, HD - 4), bf16)], axis=1
+    gains = jnp.concatenate([attention_gain, feed_gain, query_gain, key_gain])
+    gains = jnp.pad(gains, (0, HD - gains.shape[0]))[None]
+    shard = pack(
+        [query_weight, key_weight, value_weight, output_weight],
+        [gate_weight, up_weight, down_weight],
+        gains,
+        rows,
+        heads,
     )
-    weights = from_everyone(weights, FSDP).reshape(width, -1)
-    feed = jnp.concatenate([gate_weight, up_weight, down_weight], axis=1)
-    feed = lax.all_gather(feed, FSDP, axis=0, tiled=True)
+    over_zh = swapped(shard, "zh")
+    split = nq + 2 * nk + nq + HD
+    copies, feed = spread(lax.axis_index("zh").reshape(1), shard, over_zh, split, lax.axis_size(PLANE))
+    weights = lax.all_to_all(copies, PLANE, 0, 0, tiled=True).reshape(width, -1)
+    feed = lax.all_gather(feed, PLANE, axis=0, tiled=True)
     token_blocks = tp_gather(x)
-    grad_blocks = tp_gather(after(dy, token_blocks[1]))
+    grad_blocks = tp_gather(after(dy, over_zh))
+    token_blocks[3] = after(token_blocks[3], *grad_blocks)
 
     first, qraw, kraw, low, att, totals, mine, other, gains, head_gains = forward_attention(
         place, token_blocks, weights, nq, nk, cos, sin
     )
-    middle, second = middle_step(x, *tp_scatter(mine, other), gains)
+    mine, from_core, from_z, _ = tp_scatter(mine, other)
+    middle, second = middle_step(x, mine, from_core, from_z, gains)
     second_blocks = tp_gather(second)
     hidden, grad_units, mine, other = feed_step(second_blocks, grad_blocks, feed, units)
-    feed_grads = feed_weights(second_blocks, grad_blocks, grad_units, hidden)
-    mine, from_core, from_z = tp_scatter(mine, other)
-    grad_middle, branch, feed_gain_part = middle_back(
-        middle, mine, from_core, after(from_z, feed_grads), dy, gains
-    )
-    feed_sums = summed_rows(feed_grads)
-
-    branch_blocks = tp_gather(branch)
-    mine, from_core, from_z = tp_scatter(*feed_out(hidden, feed))
+    mine, from_core, from_z, passed = tp_scatter(mine, other)
+    feed_grads = feed_weights(second_blocks, grad_blocks, after(grad_units, passed), hidden)
+    from_z, feed_grads = lax.optimization_barrier((from_z, feed_grads))
+    grad_middle, branch, feed_gain_part = middle_back(middle, mine, from_core, from_z, dy, gains)
+    feed_sums = lax.psum_scatter(feed_grads, PLANE, scatter_dimension=0, tiled=True)
+    feed_sums = feed_sums.reshape(2, rows, -1)
+    take = lambda which: lax.dynamic_index_in_dim(feed_sums, which, 0, keepdims=False)
+    zh = lax.axis_index("zh")
+    feed_sums = take(zh).astype(f32) + swapped(take(1 - zh), "zh").astype(f32)
+
+    over_z = swapped(branch, "zl")
+    mine, other = feed_out(after(hidden, branch), feed)
+    branch_blocks = tp_gather(branch, after(over_z, other))
+    mine, from_core, from_z, _ = tp_scatter(mine, other)
     output = middle + mine[0].astype(f32) + from_core[0].astype(f32) + from_z.astype(f32)
     output = output.astype(bf16)
 
-    branch_blocks[3] = after(branch_blocks[3], from_core)
     grads, mine, other, branch_rows, gain_part, head_part = backward_attention(
         place, branch_blocks, token_blocks, weights, low, att, totals, qraw, kraw, cos, sin, head_gains
     )
     projection_grads = projection_weights(
         first, branch_rows, grads, att, gain_part, feed_gain_part, head_part
     )
-    mine, from_core, from_z = tp_scatter(mine, other)
+    mine, from_core, from_z, _ = tp_scatter(mine, other)
     tokens_grad = tokens_back(
-        x, mine, from_core, after(from_z, projection_grads, feed_sums, output), grad_middle, gains
+        x, mine, from_core, after(from_z, projection_grads), grad_middle, gains
     )
-    sums = summed_rows(projection_grads)
+    sums = summed_rows(after(sent_rows(projection_grads), tokens_grad, output))
 
     gain_sums = sums[:, nq + 2 * nk + nq :]
     over_z = swapped(gain_sums, "zl")

time: 401 us -> 328 us (0.82)
  waiting for transfers between devices: 211 us -> 145 us
  starting transfers between devices: 41.8 us -> 33.7 us
  Pallas kernels: 102 us -> 108 us
  local copies, waits for them, and re-layouts: 15.2 us -> 11 us
    ppermute x23 -> x26, waiting for transfers between devices: 211 us -> 106 us  [swapped(): return lax.ppermute(value, axis, [(0, 1), (1, 0)])]
    all_to_all x3 -> x2, waiting for transfers between devices: 0.01 us -> 39.1 us  [the longest x1 19.8 us: sent_rows(): lax.all_to_all(blocks, PLANE, 0, 0, tiled=True)]
    all_to_all x3 -> x2, starting transfers between devices: 31 us -> 15.1 us  [the longest x1 7.99 us: sent_rows(): lax.all_to_all(blocks, PLANE, 0, 0, tiled=True)]
    ppermute x23 -> x26, starting transfers between devices: 10.8 us -> 18.5 us  [swapped(): return lax.ppermute(value, axis, [(0, 1), (1, 0)])]
    pallas_call x0 -> x2, Pallas kernels: none -> 5.35 us  [the longest x1 3.63 us: spread(): pl.pallas_call(kernel, grid_spec=pltpu.PrefetchScalarGridSpec(num_scalar_...]
    broadcast_in_dim x8 -> x0, local copies, waits for them, and re-layouts: 4.97 us -> none  [the longest x6 3.03 us: local(): tall = lambda v: jnp.pad(v, (0, rows - v.shape[0]))[:, None]]
  transfers between devices with their start and end apart: 27 -> 30, of which waited for: 16 -> 22; matrix products, arithmetic and copies ran while one was open for 5% -> 4% of each run, Pallas kernels for 19% -> 26%
where the time goes in v3:
time: 328 us; the launch traced here: 326 us
  waiting for transfers between devices  145 us (44%)
  Pallas kernels  108 us (33%)
  starting transfers between devices  33.7 us (10%)
  other arithmetic  14.3 us (4%)
  between operations  14.2 us (4%)
  local copies, waits for them, and re-layouts  11 us (3%)
    ppermute x26, waiting for transfers between devices, swapped(): return lax.ppermute(value, axis, [(0, 1), (1, 0)])  106 us
    pallas_call x1, Pallas kernels, backward_attention(): pl.pallas_call(backward_attention_kernel, grid_spec=pltpu.PrefetchScalarG...  29.1 us
    pallas_call x1, Pallas kernels, forward_attention(): pl.pallas_call(functools.partial(forward_attention_kernel, width // lax.a...  22.9 us
    all_to_all x1, waiting for transfers between devices, sent_rows(): lax.all_to_all(blocks, PLANE, 0, 0, tiled=True)  19.8 us
    all_to_all x1, waiting for transfers between devices, local(): weights = lax.all_to_all(copies, PLANE, 0, 0, tiled=True).reshape(width, -1)  19.3 us
    ppermute x26, starting transfers between devices, swapped(): return lax.ppermute(value, axis, [(0, 1), (1, 0)])  18.5 us
    pallas_call x1, Pallas kernels, feed_step(): pl.pallas_call(feed_kernel, grid=(4,), in_specs=[*[whole((ROWS, width))]...  17.7 us
    pallas_call x1, Pallas kernels, feed_weights(): pl.pallas_call(feed_weights_kernel, grid=(width // 256,), in_specs=[*[pl....  9.96 us
  transfers between devices with their start and end apart: 30, of which 22 were waited for; matrix products, arithmetic and copies ran while one was open for 4% of the time, Pallas kernels for 26%

profile of v3, /device:TPU:28, one launch (start us, length us, event | category | flops | bytes accessed | tf_op | source)
XLA Modules:
  0.0 326.2 jit_solution(12537003260537341662)
XLA Ops:
  10.2 3.9 %collective-permute-start.3 = (bf16[32,3968]{1,0:T(8,128)(2,1)}, bf16[32,3968]{1,0:T(8,128)(2,1)S(1)}, u32[]{:S(2)}, u32[]{:S(2)}) collective-permute-start(bf16[32,3968]{1,0:T(8,128)(2,1)} %pack.1.shard), channel_id=1, source_target_pairs={{0,4},{4,0},{1,5},{5,1},{2,6},{6,2},{3,7},{7,3},{8,12},{12,8},{9,1... | collective-permute-start | bytes 761864 | tf_op jit(solution)/shard_map/ppermute | solution.py:648
  14.1 6.3 %collective-permute-done.3.other = bf16[32,3968]{1,0:T(8,128)(2,1)S(1)} collective-permute-done((bf16[32,3968]{1,0:T(8,128)(2,1)}, bf16[32,3968]{1,0:T(8,128)(2,1)S(1)}, u32[]{:S(2)}, u32[]{:S(2)}) %collective-permute-start.3) | collective-permute-done | bytes 253984 | tf_op jit(solution)/shard_map/ppermute | solution.py:648
  21.2 3.6 %spread.1 = (bf16[16,64,1664]{2,1,0:T(8,128)(2,1)}, bf16[64,2304]{1,0:T(8,128)(2,1)}) custom-call(s32[1]{0:T(128)} %bitcast.3.zh, bf16[32,3968]{1,0:T(8,128)(2,1)} %pack.1.shard, bf16[32,3968]{1,0:T(8,128)(2,1)} %copy-done.13), custom_call_target="tpu_custom_call" | custom-call | flops 125 | bytes 625000 | tf_op jit(solution)/shard_map/spread/pallas_call | solution.py:628
  24.8 7.1 %all-to-all-start = ((bf16[16,64,1664]{2,1,0:T(8,128)(2,1)}), bf16[16,64,1664]{2,1,0:T(8,128)(2,1)S(1)}, u32[]{:S(2)}, u32[]{:S(2)}) async-start(bf16[16,64,1664]{2,1,0:T(8,128)(2,1)} %get-tuple-element.53), calls=%async_computation | async-start | bytes 6815744 | tf_op jit(solution)/shard_map/all_to_all | solution.py:730
  34.1 13.1 %collective-permute-done.refs_1_.refs_5_ = bf16[256,1024]{1,0:T(8,128)(2,1)} collective-permute-done((bf16[256,1024]{1,0:T(8,128)(2,1)}, bf16[256,1024]{1,0:T(8,128)(2,1)}, u32[]{:S(2)}, u32[]{:S(2)}) %collective-permute-start) | collective-permute-done | bytes 524320 | tf_op jit(solution)/shard_map/ppermute | solution.py:648
  47.3 8.9 %collective-permute-done.4.refs_5_ = bf16[256,1024]{1,0:T(8,128)(2,1)} collective-permute-done((bf16[256,1024]{1,0:T(8,128)(2,1)}, bf16[256,1024]{1,0:T(8,128)(2,1)}, u32[]{:S(2)}, u32[]{:S(2)}) %collective-permute-start.4) | collective-permute-done | bytes 524320 | tf_op jit(solution)/shard_map/ppermute | solution.py:648
  59.2 19.3 %all-to-all-done = bf16[16,64,1664]{2,1,0:T(8,128)(2,1)S(1)} async-done(((bf16[16,64,1664]{2,1,0:T(8,128)(2,1)}), bf16[16,64,1664]{2,1,0:T(8,128)(2,1)S(1)}, u32[]{:S(2)}, u32[]{:S(2)}) %all-to-all-start) | async-done | bytes 3407904 | tf_op jit(solution)/shard_map/all_to_all | solution.py:730
  80.3 22.9 %forward_attention.1 = (bf16[1024,1024]{1,0:T(8,128)(2,1)}, f32[1024,512]{1,0:T(8,128)}, f32[1024,256]{1,0:T(8,128)}, bf16[1024,1024]{1,0:T(8,128)(2,1)}, bf16[1...) custom-call(s32[4]{0:T(128)} %fusion.8.place, ...), custom_call_target="tpu_custom_call" | custom-call | flops 875000000 | bytes 2000000 | tf_op jit(solution)/shard_map/forward_attention/pallas_call | solution.py:206
  103.3 2.9 collective-permute-done.7.from_core
  108.7 13.1 %collective-permute-done.8.from_z = bf16[256,1024]{1,0:T(8,128)(2,1)S(1)} collective-permute-done((bf16[256,1024]{1,0:T(8,128)(2,1)S(1)}, bf16[256,1024]{1,0:T(8,128)(2,1)S(1)}, u32[]{:S(2)}, u32[]{:S(2)}) %collective-permute-start.8) | collective-permute-done | bytes 524320 | tf_op jit(solution)/shard_map/ppermute | solution.py:648
  122.6 2.8 middle_step.1
  126.2 12.5 %collective-permute-done.9.refs_1_ = bf16[256,1024]{1,0:T(8,128)(2,1)S(1)} collective-permute-done((bf16[256,1024]{1,0:T(8,128)(2,1)}, bf16[256,1024]{1,0:T(8,128)(2,1)S(1)}, u32[]{:S(2)}, u32[]{:S(2)}) %collective-permute-start.9) | collective-permute-done | bytes 524320 | tf_op jit(solution)/shard_map/ppermute | solution.py:648
  141.4 17.7 %feed_step.1 = (bf16[1024,768]{1,0:T(8,128)(2,1)}, bf16[1024,1536]{1,0:T(8,128)(2,1)}, bf16[2,256,1024]{2,1,0:T(8,128)(2,1)}, bf16[2,256,1024]{2,1,0:T(8,128)(2,1)}) custom-call(bf16[256,1024]{1,0:T(8,128)(2,1)} %get-tuple-element.58.refs_0_, bf16[256,1024]{1,0:T(8,128)(2,1)} %copy-done.4, bf16[256,1024]{1,0:T(8,128)(2,1)} %copy-done.5, ...), custom_call_target="tpu_custom_call" | custom-call | flops 1000000000 | bytes 2000000 | tf_op jit(solution)/shard_map/feed_step/pallas_call | solution.py:285
  159.2 2.7 collective-permute-done.12.from_core
  164.6 10.0 %feed_weights.1 = bf16[1024,2304]{1,0:T(8,128)(2,1)} custom-call(bf16[256,1024]{1,0:T(8,128)(2,1)} %get-tuple-element.58.refs_0_, bf16[256,1024]{1,0:T(8,128)(2,1)} %copy-done.4, bf16[256,1024]{1,0:T(8,128)(2,1)} %copy-done.5, bf16[256,1024]{1,0:T(8,128)(2,1)} %copy-done.6, bf16[256,1024]{1,0:T(8,128)(2,1)} %bitcast.49, ...), custom_call_target="tpu_custom_call" | custom-call | flops 600000000 | bytes 1750000 | tf_op jit(solution)/shard_map/feed_weights/pallas_call | solution.py:346
  174.6 3.1 collective-permute-done.13.from_z
  178.5 3.1 middle_back.1
  182.6 5.7 %feed_out.1 = (bf16[2,256,1024]{2,1,0:T(8,128)(2,1)}, bf16[2,256,1024]{2,1,0:T(8,128)(2,1)}) custom-call(bf16[1024,768]{1,0:T(8,128)(2,1)} %get-tuple-element.67.refs_9_.hidden, bf16[1024,2304]{1,0:T(8,128)(2,1)} %all-gather.2.cloned.1.call-done.refs_8_.refs_9_.refs_10_.wd), custom_call_target="tpu_custom_call" | custom-call | flops 200000000 | bytes 625000 | tf_op jit(solution)/shard_map/feed_out/pallas_call | solution.py:314
  188.3 6.8 %collective-permute-done.16.refs_1_ = bf16[256,1024]{1,0:T(8,128)(2,1)S(1)} collective-permute-done((bf16[256,1024]{1,0:T(8,128)(2,1)}, bf16[256,1024]{1,0:T(8,128)(2,1)S(1)}, u32[]{:S(2)}, u32[]{:S(2)}) %collective-permute-start.16) | collective-permute-done | bytes 524320 | tf_op jit(solution)/shard_map/ppermute | solution.py:648
  197.7 29.1 %backward_attention.1 = (bf16[1024,1024]{1,0:T(8,128)(2,1)}, bf16[2,256,1024]{2,1,0:T(8,128)(2,1)}, bf16[2,256,1024]{2,1,0:T(8,128)(2,1)}, bf16[1024,1024]{1,0:T...) custom-call(s32[4]{0:T(128)} %fusion.8.place, bf16[256,1024]{1,0:T(8,128)(2,1)} %get-tuple-element.66.refs_0_, ...), custom_call_target="tpu_custom_call" | custom-call | flops 1124999936 | bytes 2250000 | tf_op jit(solution)/shard_map/backward_attention/pallas_call | solution.py:484
  226.8 8.3 %projection_weights.1 = bf16[1024,1664]{1,0:T(8,128)(2,1)} custom-call(bf16[1024,1024]{1,0:T(8,128)(2,1)} %get-tuple-element.79.first, bf16[1024,1024]{1,0:T(8,128)(2,1)} %get-tuple-element.80.branch, bf16[1024,1024]{1,0:T(8,128)(2,1)} %get-tuple-element.81.grads, bf16[1024,512]{1,0:T(8,128)(2,1)} %get-tuple-element.72.refs_11_.att, ...), custom_call_target="tpu_custom_call" | custom-call | flops 400000000 | bytes 1250000 | tf_op jit(solution)/shard_map/projection_weights/pallas_call | solution.py:539
  235.2 8.0 %all-to-all-start.1 = ((bf16[16,64,1664]{2,1,0:T(8,128)(2,1)}), bf16[16,64,1664]{2,1,0:T(8,128)(2,1)S(1)}, u32[]{:S(2)}, u32[]{:S(2)}) async-start(bf16[16,64,1664]{2,1,0:T(8,128)(2,1)} %bitcast.39), calls=%async_computation.1 | async-start | bytes 6815744 | tf_op jit(solution)/shard_map/all_to_all | solution.py:670
  253.5 10.0 %collective-permute-done.15 = bf16[256,1024]{1,0:T(8,128)(2,1)} collective-permute-done((bf16[256,1024]{1,0:T(8,128)(2,1)}, bf16[256,1024]{1,0:T(8,128)(2,1)}, u32[]{:S(2)}, u32[]{:S(2)}) %collective-permute-start.15) | collective-permute-done | bytes 524320 | tf_op jit(solution)/shard_map/ppermute | solution.py:648
  263.5 2.8 fusion.1
  266.3 7.7 %collective-permute-done.20.from_z = bf16[256,1024]{1,0:T(8,128)(2,1)} collective-permute-done((bf16[256,1024]{1,0:T(8,128)(2,1)}, bf16[256,1024]{1,0:T(8,128)(2,1)}, u32[]{:S(2)}, u32[]{:S(2)}) %collective-permute-start.20) | collective-permute-done | bytes 524320 | tf_op jit(solution)/shard_map/ppermute | solution.py:648
  273.9 2.9 tokens_back.1
  276.9 19.8 %all-to-all-done.1 = bf16[16,64,1664]{2,1,0:T(8,128)(2,1)S(1)} async-done(((bf16[16,64,1664]{2,1,0:T(8,128)(2,1)}), bf16[16,64,1664]{2,1,0:T(8,128)(2,1)S(1)}, u32[]{:S(2)}, u32[]{:S(2)}) %all-to-all-start.1) | async-done | bytes 3407904 | tf_op jit(solution)/shard_map/all_to_all | solution.py:670
  297.6 2.5 collective-permute-start.21
  300.3 3.8 %collective-permute-done.21 = bf16[32,1664]{1,0:T(8,128)(2,1)S(1)} collective-permute-done((bf16[32,1664]{1,0:T(8,128)(2,1)}, bf16[32,1664]{1,0:T(8,128)(2,1)S(1)}, u32[]{:S(2)}, u32[]{:S(2)}) %collective-permute-start.21) | collective-permute-done | bytes 106528 | tf_op jit(solution)/shard_map/ppermute | solution.py:648
  305.2 2.9 collective-permute-done.22
  310.2 2.5 collective-permute-start.25
  314.1 3.6 %collective-permute-done.25 = bf16[32,2304]{1,0:T(8,128)(2,1)S(1)} collective-permute-done((bf16[32,2304]{1,0:T(8,128)(2,1)S(1)}, bf16[32,2304]{1,0:T(8,128)(2,1)S(1)}, u32[]{:S(2)}, u32[]{:S(2)}) %collective-permute-start.25) | collective-permute-done | bytes 147488 | tf_op jit(solution)/shard_map/ppermute | solution.py:648
  (88 shorter events, 42.7 us)
Async XLA Ops:
  7.2 133.4 %all-gather.2.cloned.1.call-start = ((), (), s32[]{:S(2)}) async-start(), calls=%async_computation.3 | async-start | bytes 5013504 | tf_op jit(solution)/shard_map/all_gather | solution.py:731
  10.2 10.2 %collective-permute-start.3 = (bf16[32,3968]{1,0:T(8,128)(2,1)}, bf16[32,3968]{1,0:T(8,128)(2,1)S(1)}, u32[]{:S(2)}, u32[]{:S(2)}) collective-permute-start(bf16[32,3968]{1,0:T(8,128)(2,1)} %pack.1.shard), channel_id=1, source_target_pairs={{0,4},{4,0},{1,5},{5,1},{2,6},{6,2},{3,7},{7,3},{8,12},{12,8},{9,1... | collective-permute-start | bytes 761864 | tf_op jit(solution)/shard_map/ppermute | solution.py:648
  24.8 53.7 %all-to-all-start = ((bf16[16,64,1664]{2,1,0:T(8,128)(2,1)}), bf16[16,64,1664]{2,1,0:T(8,128)(2,1)S(1)}, u32[]{:S(2)}, u32[]{:S(2)}) async-start(bf16[16,64,1664]{2,1,0:T(8,128)(2,1)} %get-tuple-element.53), calls=%async_computation | async-start | bytes 6815744 | tf_op jit(solution)/shard_map/all_to_all | solution.py:730
  32.0 277.3 %reduce-scatter.2.cloned.1.call-start = ((), (), s32[]{:S(2)}) async-start(), calls=%async_computation.4 | async-start | bytes 5013504 | tf_op jit(solution)/shard_map/reduce_scatter | solution.py:747
  32.0 15.3 %collective-permute-start = (bf16[256,1024]{1,0:T(8,128)(2,1)}, bf16[256,1024]{1,0:T(8,128)(2,1)}, u32[]{:S(2)}, u32[]{:S(2)}) collective-permute-start(bf16[256,1024]{1,0:T(8,128)(2,1)} %bitcast.40), channel_id=1, source_target_pairs={{0,2},{2,0},{1,3},{3,1},{4,6},{6,4},{5,7},{7,5},{8,10},{10,8},{9,1... | collective-permute-start | bytes 1572872 | tf_op jit(solution)/shard_map/ppermute | solution.py:648
  33.4 22.8 %collective-permute-start.4 = (bf16[256,1024]{1,0:T(8,128)(2,1)}, bf16[256,1024]{1,0:T(8,128)(2,1)}, u32[]{:S(2)}, u32[]{:S(2)}) collective-permute-start(bf16[256,1024]{1,0:T(8,128)(2,1)} %bitcast.46), channel_id=1, source_target_pairs={{0,2},{2,0},{1,3},{3,1},{4,6},{6,4},{5,7},{7,5},{8,10},{10,8},{9,1... | collective-permute-start | bytes 1572872 | tf_op jit(solution)/shard_map/ppermute | solution.py:648
  34.1 23.1 %collective-permute-start.5 = (bf16[256,1024]{1,0:T(8,128)(2,1)}, bf16[256,1024]{1,0:T(8,128)(2,1)}, u32[]{:S(2)}, u32[]{:S(2)}) collective-permute-start(bf16[256,1024]{1,0:T(8,128)(2,1)} %bitcast.47), channel_id=1, source_target_pairs={{0,1},{1,0},{2,3},{3,2},{4,5},{5,4},{6,7},{7,6},{8,9},{9,8},{10,11... | collective-permute-start | bytes 1572872 | tf_op jit(solution)/shard_map/ppermute | solution.py:648
  47.3 9.9 %collective-permute-start.2 = (bf16[256,1024]{1,0:T(8,128)(2,1)}, bf16[256,1024]{1,0:T(8,128)(2,1)}, u32[]{:S(2)}, u32[]{:S(2)}) collective-permute-start(bf16[256,1024]{1,0:T(8,128)(2,1)} %collective-permute-done.refs_1_.refs_5_), channel_id=1, source_target_pairs={{0,1},{1,0},{2,3},{3,2},{4,5},{5,4},{6,7},{7,6},{8,9},{9,8},{10,11... | collective-permute-start | bytes 1572872 | tf_op jit(solution)/shard_map/ppermute | solution.py:648
  56.2 2.3 collective-permute-start.6
  56.2 3.0 collective-permute-start.1
  103.2 3.0 collective-permute-start.7
  106.1 15.6 %copy-start.2 = (bf16[2,256,1024]{2,1,0:T(8,128)(2,1)}, bf16[2,256,1024]{2,1,0:T(8,128)(2,1)S(1)}, u32[]{:S(2)}) copy-start(bf16[2,256,1024]{2,1,0:T(8,128)(2,1)S(1)} %collective-permute-done.7.from_core) | copy-start | bytes 3145732
  107.7 14.0 %collective-permute-start.8 = (bf16[256,1024]{1,0:T(8,128)(2,1)S(1)}, bf16[256,1024]{1,0:T(8,128)(2,1)S(1)}, u32[]{:S(2)}, u32[]{:S(2)}) collective-permute-start(bf16[256,1024]{1,0:T(8,128)(2,1)S(1)} %fusion.2), channel_id=1, source_target_pairs={{0,2},{2,0},{1,3},{3,1},{4,6},{6,4},{5,7},{7,5},{8,10},{10,8},{9,1... | collective-permute-start | bytes 1572872 | tf_op jit(solution)/shard_map/ppermute | solution.py:648
  125.3 13.3 %collective-permute-start.9 = (bf16[256,1024]{1,0:T(8,128)(2,1)}, bf16[256,1024]{1,0:T(8,128)(2,1)S(1)}, u32[]{:S(2)}, u32[]{:S(2)}) collective-permute-start(bf16[256,1024]{1,0:T(8,128)(2,1)} %get-tuple-element.58.refs_0_), channel_id=1, source_target_pairs={{0,2},{2,0},{1,3},{3,1},{4,6},{6,4},{5,7},{7,5},{8,10},{10,8},{9,1... | collective-permute-start | bytes 1572872 | tf_op jit(solution)/shard_map/ppermute | solution.py:648
  126.2 12.5 %collective-permute-start.10 = (bf16[256,1024]{1,0:T(8,128)(2,1)}, bf16[256,1024]{1,0:T(8,128)(2,1)S(1)}, u32[]{:S(2)}, u32[]{:S(2)}) collective-permute-start(bf16[256,1024]{1,0:T(8,128)(2,1)} %get-tuple-element.58.refs_0_), channel_id=1, source_target_pairs={{0,1},{1,0},{2,3},{3,2},{4,5},{5,4},{6,7},{7,6},{8,9},{9,8},{10,11... | collective-permute-start | bytes 1572872 | tf_op jit(solution)/shard_map/ppermute | solution.py:648
  138.7 1.9 collective-permute-start.11
  159.0 2.9 collective-permute-start.12
  161.9 12.7 %copy-start.3 = (bf16[2,256,1024]{2,1,0:T(8,128)(2,1)}, bf16[2,256,1024]{2,1,0:T(8,128)(2,1)S(1)}, u32[]{:S(2)}) copy-start(bf16[2,256,1024]{2,1,0:T(8,128)(2,1)S(1)} %collective-permute-done.12.from_core) | copy-start | bytes 3145732
  163.5 14.2 %collective-permute-start.13 = (bf16[256,1024]{1,0:T(8,128)(2,1)S(1)}, bf16[256,1024]{1,0:T(8,128)(2,1)S(1)}, u32[]{:S(2)}, u32[]{:S(2)}) collective-permute-start(bf16[256,1024]{1,0:T(8,128)(2,1)S(1)} %fusion.3), channel_id=1, source_target_pairs={{0,2},{2,0},{1,3},{3,1},{4,6},{6,4},{5,7},{7,5},{8,10},{10,8},{9,1... | collective-permute-start | bytes 1572872 | tf_op jit(solution)/shard_map/ppermute | solution.py:648
  181.6 13.4 %collective-permute-start.16 = (bf16[256,1024]{1,0:T(8,128)(2,1)}, bf16[256,1024]{1,0:T(8,128)(2,1)S(1)}, u32[]{:S(2)}, u32[]{:S(2)}) collective-permute-start(bf16[256,1024]{1,0:T(8,128)(2,1)} %get-tuple-element.66.refs_0_), channel_id=1, source_target_pairs={{0,2},{2,0},{1,3},{3,1},{4,6},{6,4},{5,7},{7,5},{8,10},{10,8},{9,1... | collective-permute-start | bytes 1572872 | tf_op jit(solution)/shard_map/ppermute | solution.py:648
  182.6 12.5 %collective-permute-start.17 = (bf16[256,1024]{1,0:T(8,128)(2,1)}, bf16[256,1024]{1,0:T(8,128)(2,1)S(1)}, u32[]{:S(2)}, u32[]{:S(2)}) collective-permute-start(bf16[256,1024]{1,0:T(8,128)(2,1)} %get-tuple-element.66.refs_0_), channel_id=1, source_target_pairs={{0,1},{1,0},{2,3},{3,2},{4,5},{5,4},{6,7},{7,6},{8,9},{9,8},{10,11... | collective-permute-start | bytes 1572872 | tf_op jit(solution)/shard_map/ppermute | solution.py:648
  195.0 1.9 collective-permute-start.18
  235.2 61.5 %all-to-all-start.1 = ((bf16[16,64,1664]{2,1,0:T(8,128)(2,1)}), bf16[16,64,1664]{2,1,0:T(8,128)(2,1)S(1)}, u32[]{:S(2)}, u32[]{:S(2)}) async-start(bf16[16,64,1664]{2,1,0:T(8,128)(2,1)} %bitcast.39), calls=%async_computation.1 | async-start | bytes 6815744 | tf_op jit(solution)/shard_map/all_to_all | solution.py:670
  243.2 2.9 collective-permute-start.14
  243.2 6.0 %collective-permute-start.19 = (bf16[2,256,1024]{2,1,0:T(8,128)(2,1)}, bf16[2,256,1024]{2,1,0:T(8,128)(2,1)S(1)}, u32[]{:S(2)}, u32[]{:S(2)}) collective-permute-start(bf16[2,256,1024]{2,1,0:T(8,128)(2,1)} %get-tuple-element.78), channel_id=1, source_target_pairs={{0,1},{1,0},{2,3},{3,2},{4,5},{5,4},{6,7},{7,6},{8,9},{9,8},{10,11... | collective-permute-start | bytes 3145736 | tf_op jit(solution)/shard_map/ppermute | solution.py:648
  248.4 15.1 %collective-permute-start.15 = (bf16[256,1024]{1,0:T(8,128)(2,1)}, bf16[256,1024]{1,0:T(8,128)(2,1)}, u32[]{:S(2)}, u32[]{:S(2)}) collective-permute-start(bf16[256,1024]{1,0:T(8,128)(2,1)} %fusion.4), channel_id=1, source_target_pairs={{0,2},{2,0},{1,3},{3,1},{4,6},{6,4},{5,7},{7,5},{8,10},{10,8},{9,1... | collective-permute-start | bytes 1572872 | tf_op jit(solution)/shard_map/ppermute | solution.py:648
  252.2 21.8 %collective-permute-start.20 = (bf16[256,1024]{1,0:T(8,128)(2,1)}, bf16[256,1024]{1,0:T(8,128)(2,1)}, u32[]{:S(2)}, u32[]{:S(2)}) collective-permute-start(bf16[256,1024]{1,0:T(8,128)(2,1)} %fusion.5), channel_id=1, source_target_pairs={{0,2},{2,0},{1,3},{3,1},{4,6},{6,4},{5,7},{7,5},{8,10},{10,8},{9,1... | collective-permute-start | bytes 1572872 | tf_op jit(solution)/shard_map/ppermute | solution.py:648
  297.6 6.5 %collective-permute-start.21 = (bf16[32,1664]{1,0:T(8,128)(2,1)}, bf16[32,1664]{1,0:T(8,128)(2,1)S(1)}, u32[]{:S(2)}, u32[]{:S(2)}) collective-permute-start(bf16[32,1664]{1,0:T(8,128)(2,1)} %dynamic-slice_reduce_fusion), channel_id=1, source_target_pairs={{0,4},{4,0},{1,5},{5,1},{2,6},{6,2},{3,7},{7,3},{8,12},{12,8},{9,1... | collective-permute-start | bytes 319496 | tf_op jit(solution)/shard_map/ppermute | solution.py:648
  304.1 4.5 %collective-permute-start.23 = (f32[32,128]{1,0:T(8,128)S(1)}, f32[32,128]{1,0:T(8,128)S(1)}, u32[]{:S(2)}, u32[]{:S(2)}) collective-permute-start(f32[32,128]{1,0:T(8,128)S(1)} %slice.93), channel_id=1, source_target_pairs={{0,1},{1,0},{2,3},{3,2},{4,5},{5,4},{6,7},{7,6},{8,9},{9,8},{10,11... | collective-permute-start | bytes 49160 | tf_op jit(solution)/shard_map/ppermute | solution.py:648
  304.2 3.8 %collective-permute-start.22 = (f32[32,128]{1,0:T(8,128)S(1)}, f32[32,128]{1,0:T(8,128)S(1)}, u32[]{:S(2)}, u32[]{:S(2)}) collective-permute-start(f32[32,128]{1,0:T(8,128)S(1)} %slice.93), channel_id=1, source_target_pairs={{0,2},{2,0},{1,3},{3,1},{4,6},{6,4},{5,7},{7,5},{8,10},{10,8},{9,1... | collective-permute-start | bytes 49160 | tf_op jit(solution)/shard_map/ppermute | solution.py:648
  308.1 1.2 collective-permute-start.24
  310.2 7.5 %collective-permute-start.25 = (bf16[32,2304]{1,0:T(8,128)(2,1)S(1)}, bf16[32,2304]{1,0:T(8,128)(2,1)S(1)}, u32[]{:S(2)}, u32[]{:S(2)}) collective-permute-start(bf16[32,2304]{1,0:T(8,128)(2,1)S(1)} %dynamic-slice_bitcast_fusion), channel_id=1, source_target_pairs={{0,4},{4,0},{1,5},{5,1},{2,6},{6,2},{3,7},{7,3},{8,12},{12,8},{9,1... | collective-permute-start | bytes 442376 | tf_op jit(solution)/shard_map/ppermute | solution.py:648
  (12 other events, 20.5 us)
Sparse Core Ops, SparseCore 0:
  24.9 81.8 all-gather.1
  177.9 107.9 reduce-scatter.1
